TPU v7x, 128 devices: a whole 4x4x4 slice. The times are simulated.
128 devices in a mesh: gx: 8 (over z, core), gy: 16 (over x, y).
Axes of the slice: x: 4, y: 4, z: 4, core: 2. Of those that a mesh axis runs over, the one named last changes fastest.
Arguments:
- forward_fields: bfloat16 [2, 3, 3, 8, 768, 6144], P(None, None, None, None, 'gx', 'gy'), may hold values from -6 to 6
- adjoint_fields: bfloat16 [2, 3, 3, 8, 768, 6144], P(None, None, None, None, 'gx', 'gy'), may hold values from -6 to 6
- wave_weights: float32 [2, 3], replicated, may hold values from -4 to 4
- density: float32 [8, 512, 4096], P(None, 'gx', 'gy'), may hold values from 0 to 1
- row_edges: int32 [9], replicated, may hold values from 0 to 512, as said below
- column_edges: int32 [17], replicated, may hold values from 0 to 4096, as said below
Outputs:
- design_gradient: float32 [8, 512, 4096], P(None, 'gx', 'gy')
Inputs may be any that keep to these rules, and one draw needn't show every extreme that they name: row_edges rises from 0 to 512; entry i lies within 16 of i * 64, so every group spans 32 to 96 cells along x, and some group spans exactly 96. column_edges rises from 0 to 4096; entry j lies within 64 of j * 256, so every group spans 128 to 384 cells along y, and some group spans exactly 384.
All inputs are finite; a program needn't handle non-finite values.
Results may differ from a plain program's by a relative error of at most 0.0003.
Values sent between devices are 32-bit elements; how exact they have to be, the bound alone decides.
No kernel may reach another device: no remote copies, remote signals or barrier semaphores. Data moves between devices by JAX's collectives and lax.ppermute only.
A program may use at most 192 MiB of HBM per device.

v0:
```python
import jax
import jax.numpy as jnp
import ml_dtypes
import numpy as np
from jax import lax
from jax.experimental import pallas as pl
from jax.experimental.pallas import tpu as pltpu
from jax.sharding import PartitionSpec as P

RADIUS = 10
SETTINGS = 10
REACH = RADIUS - 1
TAPS = 2 * REACH + 1
BETA = 64.0
ETA = 0.5
LANES = 128
LAYERS = 8
LAGS = (TAPS + 1) // 2
ROWS, COLS = 64, 256
GROUP_ROWS, GROUP_COLS = 96, 384
ROW_SLACK, COL_SLACK = 16, 64
FRAME_ROWS = GROUP_ROWS + 2 * ROW_SLACK
SIDE = ROW_SLACK + REACH
FIRST = ROW_SLACK - REACH
NEED = ROWS + 2 * REACH
HALO = 2 * REACH
NINES = LANES // REACH
GROUPED = (ROWS + 2 * HALO) // 4
SPAN = LANES - 2 * REACH
SLOPE_PAIRS = NEED // 2 + 1
DENSITY_PAIRS = (NEED + HALO) // 2 + 2
F32 = jnp.float32
BF16 = jnp.bfloat16


def cone_blocks():
    offsets = np.arange(-RADIUS, RADIUS + 1).astype(np.float64)
    cone = np.maximum(1.0 - np.sqrt(offsets[:, None] ** 2 + offsets[None, :] ** 2) / RADIUS, 0.0)
    cone = (cone / cone.sum())[1:-1, 1:-1]
    blocks = np.zeros((LAGS, 2, LANES, 2, LANES))
    lanes = np.arange(REACH, LANES - REACH)
    for lag in range(LAGS):
        for source in range(2):
            for target in range(2):
                a = 2 * lag + source - target
                if 0 <= a < TAPS:
                    for b in range(TAPS):
                        blocks[lag, source, lanes + b - REACH, target, lanes] = cone[a, b]
    blocks = blocks.reshape(LAGS * 2 * LANES, 2 * LANES)
    high = blocks.astype(ml_dtypes.bfloat16)
    low = (blocks - high.astype(np.float64)).astype(ml_dtypes.bfloat16)
    return high, low


def lane_of(rows):
    return lax.broadcasted_iota(jnp.int32, (rows, LANES), 1)


def turn(value, shift):
    return pltpu.roll(value, shift % LANES, 1)


def place():
    i, j = lax.axis_index("gx"), lax.axis_index("gy")
    return i, j, lax.rem(i, 2), lax.rem(j, 2)


def sides_of():
    i, j = lax.axis_index("gx"), lax.axis_index("gy")
    return i > 0, i < lax.axis_size("gx") - 1, j > 0, j < lax.axis_size("gy") - 1


def chosen(parity, first, second):
    return jnp.where(parity == 0, first, second)


def row_at(e):
    return slice(e * LAYERS, (e + 1) * LAYERS)


def pair_at(e):
    return row_at(e // 2), slice((e % 2) * LANES, (e % 2 + 1) * LANES)


def start_kernel(flat, weights, rows, cols, xe, xo, tiles, settings, w_smem, r_smem, c_smem, sems):
    i, j, pi, pj = place()
    copies = [
        pltpu.make_async_copy(flat.at[:, 0:LANES], tiles.at[0], sems.at[0]),
        pltpu.make_async_copy(flat.at[:, LANES:COLS], tiles.at[1], sems.at[1]),
        pltpu.make_async_copy(weights, w_smem, sems.at[2]),
        pltpu.make_async_copy(rows, r_smem, sems.at[3]),
        pltpu.make_async_copy(cols, c_smem, sems.at[4]),
    ]
    for copy in copies:
        copy.start()
    for copy in copies:
        copy.wait()
    settings[0] = (r_smem[i] - i * ROWS + ROW_SLACK).astype(F32)
    settings[1] = (c_smem[j] - j * COLS + COL_SLACK).astype(F32)
    settings[2] = (r_smem[i + 1] - r_smem[i]).astype(F32)
    settings[3] = (c_smem[j + 1] - c_smem[j]).astype(F32)
    for part in range(2):
        for w in range(3):
            settings[4 + 3 * part + w] = w_smem[part, w]
    for parity, out in ((0, xe), (1, xo)):
        start = jnp.where(pi == parity, ROWS - HALO, 0)
        for r in range(HALO):
            for k in range(2):
                out[k, row_at(r), :] = tiles[k, pl.ds(start + r, LAYERS, stride=ROWS), :]


def correlate_kernel(forward, adjoint, settings, frame, xe, xo, fields, sems):
    i, j, pi, pj = place()

    def copies(n):
        return [
            pltpu.make_async_copy(source.at[:, :, :, n], fields.at[k, :, :, :, n], sems.at[k, n])
            for k, source in enumerate((forward, adjoint))
        ]

    for n in range(LAYERS):
        for copy in copies(n):
            copy.start()
    frame[...] = jnp.zeros_like(frame)
    down, across, span_rows, span_cols = [settings[n].astype(jnp.int32) for n in range(4)]
    weights = [[settings[4 + 3 * part + w] for w in range(3)] for part in range(2)]
    lane = lane_of(16)
    row = lax.broadcasted_iota(jnp.int32, (16, LANES), 0)
    turned = lax.rem(across, LANES)

    @pl.loop(0, LAYERS)
    def _(n):
        for copy in copies(n):
            copy.wait()
        for r in range(GROUP_ROWS // 16):
            before = jnp.zeros((16, LANES), F32)
            for k in range(3):
                at = (n, slice(16 * r, 16 * r + 16), slice(LANES * k, LANES * (k + 1)))
                total = None
                for w in range(3):
                    real = imag = None
                    for c in range(3):
                        fr = fields[(0, 0, w, c) + at].astype(F32)
                        fi = fields[(0, 1, w, c) + at].astype(F32)
                        ar = fields[(1, 0, w, c) + at].astype(F32)
                        ai = fields[(1, 1, w, c) + at].astype(F32)
                        re = fr * ar - fi * ai
                        im = fr * ai + fi * ar
                        real = re if real is None else real + re
                        imag = im if imag is None else imag + im
                    term = weights[0][w] * real - weights[1][w] * imag
                    total = term if total is None else total + term
                inside = (row < span_rows - 16 * r) & (lane < span_cols - LANES * k)
                total = pltpu.roll(jnp.where(inside, total, 0.0), turned, 1)
                value = jnp.where(lane >= across, total, before)
                before = total
                frame[k, pl.ds((16 * r + down) * LAYERS + n, 16, stride=LAYERS), :] = value

    for parity, out in ((0, xe), (1, xo)):
        start = pl.multiple_of(jnp.where(pi == parity, ROWS + FIRST, 0) * LAYERS, 8)
        out[...] = frame[:, pl.ds(start, SIDE * LAYERS), :]


def density_row(tiles, xe, xo, e, k):
    i, j, pi, pj = place()
    has_up, has_down, has_left, has_right = sides_of()
    if e >= ROWS + 2 * HALO:
        return jnp.zeros((LAYERS, LANES), F32)
    if HALO <= e < HALO + ROWS:
        return tiles[k, pl.ds(e - HALO, LAYERS, stride=ROWS), :]
    at = (k, row_at(e % (HALO + ROWS)))
    if e < HALO:
        return jnp.where(has_up, chosen(pi, xo[at], xe[at]), 0.0)
    return jnp.where(has_down, chosen(pi, xe[at], xo[at]), 0.0)


def density_columns_kernel(tiles, xe, xo, ye, yo):
    i, j, pi, pj = place()
    lane = lane_of(LAYERS)
    for r in range(GROUPED):
        left = right = None
        for g in range(4):
            a = turn(density_row(tiles, xe, xo, g * GROUPED + r, 0), 32 * g)
            b = turn(density_row(tiles, xe, xo, g * GROUPED + r, 1), 32 * g + 32)
            left = a if g == 0 else jnp.where(lane >= 32 * g, a, left)
            right = b if g == 0 else jnp.where(lane >= 32 * g, b, right)
        ye[row_at(r), :] = chosen(pj, right, left)
        yo[row_at(r), :] = chosen(pj, left, right)


def split_copies(windows, copies, pairs):
    for shift in range(2):
        for g in range((pairs - shift) // 2):
            value = windows[(2 * g + shift) * LAYERS : (2 * g + shift + 2) * LAYERS, :]
            high = value.astype(BF16)
            low = (value - high.astype(F32)).astype(BF16)
            copies[shift, 0, 16 * g : 16 * g + 16, :] = high
            copies[shift, 1, 16 * g : 16 * g + 16, :] = low


def banded(windows, copies, pairs, high_ref, low_ref, rows):
    split_copies(windows, copies, pairs)

    def part(kind):
        return jnp.concatenate(
            [copies[lag % 2, kind, 16 * (lag // 2) : 16 * (lag // 2) + rows, :] for lag in range(LAGS)], axis=1
        )

    high = part(0)
    out = jnp.dot(part(1), high_ref[...], preferred_element_type=F32)
    out += jnp.dot(high, low_ref[...], preferred_element_type=F32)
    return out + jnp.dot(high, high_ref[...], preferred_element_type=F32)


def slope_of(filtered):
    e = jnp.exp(-2.0 * BETA * jnp.abs(filtered - ETA))
    scale = 4.0 * BETA / (np.tanh(BETA * ETA) + np.tanh(BETA * (1.0 - ETA)))
    return np.float32(scale) * e / ((1.0 + e) * (1.0 + e))


def slope_middle_kernel(tiles, xe, xo, high_ref, low_ref, slope, windows, copies):
    lane = lane_of(LAYERS)
    for e in range(2 * DENSITY_PAIRS):
        t0, t1 = [density_row(tiles, xe, xo, e, k) for k in range(2)]
        windows[pair_at(e)] = jnp.where(lane < 64, turn(t0, 64), turn(t1, 64))
    slope[...] = slope_of(banded(windows, copies, DENSITY_PAIRS, high_ref, low_ref, SLOPE_PAIRS * LAYERS))


def slope_sides_kernel(tiles, xe, xo, ye, yo, high_ref, low_ref, left_slope, right_slope, windows, copies):
    i, j, pi, pj = place()
    has_up, has_down, has_left, has_right = sides_of()
    lane = lane_of(LAYERS)
    for e in range(2 * DENSITY_PAIRS):
        g, r = divmod(min(e, 4 * GROUPED - 1), GROUPED)
        at = row_at(r)
        left = turn(jnp.where(has_left, chosen(pj, yo[at, :], ye[at, :]), 0.0), 28 - 14 - 32 * g)
        right = turn(jnp.where(has_right, chosen(pj, ye[at, :], yo[at, :]), 0.0), 82 - 32 * g)
        t0, t1 = [turn(density_row(tiles, xe, xo, e, k), 46 - 92 * k) for k in range(2)]
        windows[(0,) + pair_at(e)] = jnp.where(lane >= 46, t0, jnp.where(lane >= 28, left, 0.0))
        windows[(1,) + pair_at(e)] = jnp.where(lane < 82, t1, jnp.where(lane < 100, right, 0.0))
    for n, out in enumerate((left_slope, right_slope)):
        value = banded(windows.at[n], copies.at[n], DENSITY_PAIRS, high_ref, low_ref, SLOPE_PAIRS * LAYERS)
        out[...] = slope_of(value)


def side_rows(count):
    return -(-count // 2), -(-count // NINES)


def add_rows(frame, xe, xo, tiles):
    i, j, pi, pj = place()
    has_up, has_down, has_left, has_right = sides_of()
    size = SIDE * LAYERS
    for k in tiles:
        frame[k, FIRST * LAYERS : FIRST * LAYERS + size, :] += jnp.where(has_up, chosen(pi, xo[k], xe[k]), 0.0)
        frame[k, ROWS * LAYERS : ROWS * LAYERS + size, :] += jnp.where(has_down, chosen(pi, xe[k], xo[k]), 0.0)


def columns_kernel(own, xe, xo, ye, yo, frame):
    i, j, pi, pj = place()
    for k in (0, 2):
        frame[k] = own[k, 0 : GROUP_ROWS * LAYERS, :]
    add_rows(frame, xe, xo, (0, 2))
    half, nine = side_rows(NEED)
    upper, lower = lane_of(half * LAYERS), lane_of(nine * LAYERS)
    for parity, out in ((0, ye), (1, yo)):
        right = pj == parity
        tile = jnp.where(right, 2, 0)
        first = frame[tile, FIRST * LAYERS : (FIRST + half) * LAYERS, :]
        second = frame[tile, (FIRST + half) * LAYERS : (FIRST + 2 * half) * LAYERS, :]
        swing = jnp.where(right, 0, 64)
        out[0 : half * LAYERS, :] = jnp.where(upper >= 64, pltpu.roll(first, swing, 1), pltpu.roll(second, 64 - swing, 1))
        packed = jnp.zeros((nine * LAYERS, LANES), F32)
        base = jnp.where(right, LANES - 55, 64)
        for g in range(NINES):
            value = frame[tile, (FIRST + nine * g) * LAYERS : (FIRST + nine * (g + 1)) * LAYERS, :]
            value = pltpu.roll(value, lax.rem(base + REACH * g, LANES), 1)
            packed = jnp.where((lower >= REACH * g) & (lower < REACH * g + REACH), value, packed)
        out[half * LAYERS : (half + nine) * LAYERS, :] = packed


def side_unpack(frame, packed, tile, valid):
    half, nine = side_rows(NEED)
    from_left = tile == 0
    lane = lane_of(half * LAYERS)
    keep = ((lane >= 64) if from_left else (lane < 64)) & valid
    value = packed(0, half * LAYERS)
    for h in range(2):
        at = pl.ds((FIRST + h * half) * LAYERS, half * LAYERS)
        shown = turn(value, 64) if (h == 0) != from_left else value
        frame[tile, at, :] += jnp.where(keep, shown, 0.0)
    lane = lane_of(nine * LAYERS)
    value = packed(half * LAYERS, nine * LAYERS)
    start = 55 if from_left else 64
    keep = (lane >= start) & (lane < start + REACH) & valid
    for g in range(NINES):
        at = pl.ds((FIRST + nine * g) * LAYERS, nine * LAYERS)
        frame[tile, at, :] += jnp.where(keep, turn(value, start - REACH * g), 0.0)


def gradient_middle_kernel(own, xe, xo, left_slope, slope, right_slope, high_ref, low_ref, out, frame, windows, copies):
    lane = lane_of(LAYERS)
    frame[1] = own[1, 0 : GROUP_ROWS * LAYERS, :]
    add_rows(frame, xe, xo, (1,))
    for e in range(2 * SLOPE_PAIRS):
        at = pair_at(e)
        factor = jnp.where(lane < REACH, turn(left_slope[at], -SPAN), slope[at])
        factor = jnp.where(lane < LANES - REACH, factor, turn(right_slope[at], SPAN))
        windows[at] = frame[1, row_at(FIRST + e), :] * factor
    out[...] = banded(windows, copies, SLOPE_PAIRS, high_ref, low_ref, ROWS // 2 * LAYERS)


def gradient_sides_kernel(
    own, xe, xo, ye, yo, left_slope, slope, right_slope, middle, high_ref, low_ref, out, frame, windows, copies, result
):
    i, j, pi, pj = place()
    has_up, has_down, has_left, has_right = sides_of()
    frame[...] = own[:, 0 : GROUP_ROWS * LAYERS, :]
    add_rows(frame, xe, xo, range(3))

    def pick(first, second):
        return lambda at, count: chosen(pj, first[at : at + count, :], second[at : at + count, :])

    side_unpack(frame, pick(yo, ye), 0, has_left)
    side_unpack(frame, pick(ye, yo), 2, has_right)
    lane = lane_of(LAYERS)
    for e in range(2 * SLOPE_PAIRS):
        at = pair_at(e)
        t0, t1, t2 = [frame[k, row_at(FIRST + e), :] for k in range(3)]
        factor = jnp.where(lane < LANES - REACH, left_slope[at], turn(slope[at], SPAN))
        windows[(0,) + at] = jnp.where(lane < 110, turn(t0, -18), turn(t1, -18)) * factor
        factor = jnp.where(lane < REACH, turn(slope[at], -SPAN), right_slope[at])
        windows[(1,) + at] = jnp.where(lane < 18, turn(t1, 18), turn(t2, 18)) * factor
    for n in range(2):
        result[n] = banded(windows.at[n], copies.at[n], SLOPE_PAIRS, high_ref, low_ref, ROWS // 2 * LAYERS)
    for e in range(ROWS):
        at = pair_at(e)
        mid = turn(middle[at], 64)
        frame[0, row_at(e), :] = jnp.where(lane < 73, turn(result[(0,) + at], -46), mid)
        frame[1, row_at(e), :] = jnp.where(lane < 55, mid, turn(result[(1,) + at], 46))
    for z in range(LAYERS):
        for k in range(2):
            out[z, :, LANES * k : LANES * (k + 1)] = frame[k, pl.ds(z, ROWS, stride=LAYERS), :]


def partner(index, count, parity):
    other = index ^ 1 if parity == 0 else ((index - 1) ^ 1) + 1
    return other if 0 <= other < count else None


def exchange(pair, axis):
    nx, ny = lax.axis_size("gx"), lax.axis_size("gy")
    arrived = []
    for parity, value in enumerate(pair):
        moves = []
        for i in range(nx):
            for j in range(ny):
                to = (partner(i, nx, parity), j) if axis == "gx" else (i, partner(j, ny, parity))
                if None in to:
                    to = (i, j ^ 1) if axis == "gx" else (i ^ 1, j)
                moves.append((i * ny + j, to[0] * ny + to[1]))
        arrived.append(lax.ppermute(value, ("gx", "gy"), moves))
    return arrived


ANY = pl.BlockSpec(memory_space=pl.ANY)
SMEM = pl.BlockSpec(memory_space=pltpu.SMEM)
VMEM = pl.BlockSpec(memory_space=pltpu.VMEM)


def shaped(*shape):
    return jax.ShapeDtypeStruct(shape, F32)


def call(kernel, name, ins, outs, scratch, mib, flops, moved):
    return pl.pallas_call(
        kernel,
        out_shape=outs,
        in_specs=ins,
        out_specs=jax.tree.map(lambda s: SMEM if s.shape == (SETTINGS,) else VMEM, outs),
        scratch_shapes=scratch,
        compiler_params=pltpu.CompilerParams(vmem_limit_bytes=mib << 20),
        cost_estimate=pl.CostEstimate(flops=int(flops), bytes_accessed=int(moved * (1 << 20)), transcendentals=0),
        name=name,
    )


def body(forward, adjoint, weights, density, row_edges, column_edges):
    high, low = (jnp.asarray(m) for m in cone_blocks())
    forward, adjoint, flat, weights, row_edges, column_edges = [
        pltpu.with_memory_space_constraint(x, pltpu.HBM)
        for x in (forward, adjoint, density.reshape(LAYERS * ROWS, COLS), weights, row_edges, column_edges)
    ]
    halo = shaped(2, HALO * LAYERS, LANES)
    tile = shaped(2, LAYERS * ROWS, LANES)
    whole_frame = shaped(3, FRAME_ROWS * LAYERS, LANES)
    fields = pltpu.VMEM((2, 2, 3, 3, LAYERS, GROUP_ROWS, GROUP_COLS), BF16)
    sems = pltpu.SemaphoreType.DMA((2, LAYERS))
    xe, xo, tiles, settings = call(
        start_kernel,
        "start",
        [ANY] * 4,
        [halo, halo, tile, shaped(SETTINGS)],
        [
            pltpu.SMEM((2, 3), F32),
            pltpu.SMEM(row_edges.shape, jnp.int32),
            pltpu.SMEM(column_edges.shape, jnp.int32),
            pltpu.SemaphoreType.DMA((5,)),
        ],
        2,
        0,
        1,
    )(flat, weights, row_edges, column_edges)
    halo_rows = exchange((xe, xo), "gx")

    side = shaped(3, SIDE * LAYERS, LANES)
    frame, *own_rows = call(
        correlate_kernel, "correlate", [ANY, ANY, SMEM], [whole_frame, side, side], [fields, sems], 28, 0, 24
    )(forward, adjoint, settings)
    own_rows = exchange(own_rows, "gx")

    column = shaped(GROUPED * LAYERS, LANES)
    halo_columns = call(density_columns_kernel, "density_columns", [VMEM] * 3, [column, column], [], 2, 0, 30)(
        tiles, *halo_rows
    )
    halo_columns = exchange(halo_columns, "gy")

    def work(pairs, windows):
        lead = () if windows == 1 else (windows,)
        return [
            pltpu.VMEM(lead + (pairs * LAYERS, 2 * LANES), F32),
            pltpu.VMEM(lead + (2, 2, pairs * LAYERS, 2 * LANES), BF16),
        ]

    slope = shaped(SLOPE_PAIRS * LAYERS, 2 * LANES)
    middle_slope = call(
        slope_middle_kernel, "slope_middle", [VMEM] * 5, slope, work(DENSITY_PAIRS, 1), 8, 1.3e9, 30
    )(tiles, *halo_rows, high, low)
    left_slope, right_slope = call(
        slope_sides_kernel, "slope_sides", [VMEM] * 7, [slope, slope], work(DENSITY_PAIRS, 2), 8, 2.6e9, 4
    )(tiles, *halo_rows, *halo_columns, high, low)

    own_frame = pltpu.VMEM((3, GROUP_ROWS * LAYERS, LANES), F32)
    packed = shaped(sum(side_rows(NEED)) * LAYERS, LANES)
    own_columns = call(columns_kernel, "columns", [VMEM] * 3, [packed, packed], [own_frame], 4, 0, 4)(frame, *own_rows)
    own_columns = exchange(own_columns, "gy")

    middle = call(
        gradient_middle_kernel,
        "gradient_middle",
        [VMEM] * 8,
        shaped(ROWS // 2 * LAYERS, 2 * LANES),
        [own_frame] + work(SLOPE_PAIRS, 1),
        8,
        1e9,
        4,
    )(frame, *own_rows, left_slope, middle_slope, right_slope, high, low)
    return call(
        gradient_sides_kernel,
        "gradient_sides",
        [VMEM] * 11,
        shaped(*density.shape),
        [own_frame] + work(SLOPE_PAIRS, 2) + [pltpu.VMEM((2, ROWS // 2 * LAYERS, 2 * LANES), F32)],
        12,
        2e9,
        4,
    )(frame, *own_rows, *own_columns, left_slope, middle_slope, right_slope, middle, high, low)


def solution(mesh):
    placed = (
        P(None, None, None, None, "gx", "gy"),
        P(None, None, None, None, "gx", "gy"),
        P(),
        P(None, "gx", "gy"),
        P(),
        P(),
    )
    return jax.shard_map(body, mesh=mesh, in_specs=placed, out_specs=P(None, "gx", "gy"), check_vma=False)
```

profile of v0, /device:TPU:2, one launch (start us, length us, event | category | flops | bytes accessed | tf_op | source)
XLA Modules:
  0.0 38.7 jit_solution(1904279651698593557)
XLA Ops:
  0.0 1.9 %start.1 = (f32[2,144,128]{2,1,0:T(8,128)S(1)}, f32[2,144,128]{2,1,0:T(8,128)S(1)}, f32[2,512,128]{2,1,0:T(8,128)S(1)}, f32[10]{0:T(128)S(1)}) custom-call(f32[512,256]{1,0:T(8,128)} %bitcast.1, f32[2,3]{1,0:T(2,128)} %weights.1, s32[9]{0:T(128)} %rows.1, s32[17]{0:T(128)} %cols.1), custom_call_target="tpu_custom_call" | custom-call | bytes 1048576 | tf_op jit(solution)/shard_map/start/pallas_call | solution.py:399
  1.9 0.0 copy-start
  1.9 0.0 copy-start.1
  1.9 8.7 %correlate.1 = (f32[3,1024,128]{2,1,0:T(8,128)S(1)}, f32[3,200,128]{2,1,0:T(8,128)S(1)}, f32[3,200,128]{2,1,0:T(8,128)S(1)}) custom-call(bf16[2,3,3,8,96,384]{5,4,3,2,1,0:T(8,128)(2,1)} %forward.1, bf16[2,3,3,8,96,384]{5,4,3,2,1,0:T(8,128)(2,1)} %adjoint.1, f32[10]{0:T(128)S(1)} %get-tuple-element.18.settings), custom_call_target="tpu_custom_call" | custom-call | bytes 25165824 | tf_op jit(solution)/shard_map/correlate/pallas_call | solution.py:417
  10.6 0.1 collective-permute-start
  10.7 1.7 %collective-permute-start.1 = (f32[3,200,128]{2,1,0:T(8,128)S(1)}, f32[3,200,128]{2,1,0:T(8,128)S(1)}, u32[]{:S(2)}, u32[]{:S(2)}) collective-permute-start(f32[3,200,128]{2,1,0:T(8,128)S(1)} %get-tuple-element.21), channel_id=1, source_target_pairs={{0,1},{1,0},{2,3},{3,2},{4,5},{5,4},{6,7},{7,6},{8,9},{9,8},{10,11... | collective-permute-start | bytes 921608 | tf_op jit(solution)/shard_map/ppermute | solution.py:362
  12.3 0.5 %collective-permute-start.4 = (f32[2,144,128]{2,1,0:T(8,128)S(1)}, f32[2,144,128]{2,1,0:T(8,128)S(1)}, u32[]{:S(2)}, u32[]{:S(2)}) collective-permute-start(f32[2,144,128]{2,1,0:T(8,128)S(1)} %get-tuple-element.25), channel_id=1, source_target_pairs={{0,16},{1,17},{2,18},{3,19},{4,20},{5,21},{6,22},{7,23},{8,24},{9,... | collective-permute-start | bytes 442376 | tf_op jit(solution)/shard_map/ppermute | solution.py:362
  12.8 1.6 %collective-permute-start.5 = (f32[2,144,128]{2,1,0:T(8,128)S(1)}, f32[2,144,128]{2,1,0:T(8,128)S(1)}, u32[]{:S(2)}, u32[]{:S(2)}) collective-permute-start(f32[2,144,128]{2,1,0:T(8,128)S(1)} %get-tuple-element.26), channel_id=1, source_target_pairs={{0,1},{1,0},{2,3},{3,2},{4,5},{5,4},{6,7},{7,6},{8,9},{9,8},{10,11... | collective-permute-start | bytes 442376 | tf_op jit(solution)/shard_map/ppermute | solution.py:362
  14.4 0.0 collective-permute-done.4.xe
  14.4 4.8 %collective-permute-done.5.xo = f32[2,144,128]{2,1,0:T(8,128)S(1)} collective-permute-done((f32[2,144,128]{2,1,0:T(8,128)S(1)}, f32[2,144,128]{2,1,0:T(8,128)S(1)}, u32[]{:S(2)}, u32[]{:S(2)}) %collective-permute-start.5) | collective-permute-done | bytes 147488 | tf_op jit(solution)/shard_map/ppermute | solution.py:362
  19.2 0.4 density_columns.1
  19.6 1.7 %collective-permute-start.6 = (f32[200,128]{1,0:T(8,128)S(1)}, f32[200,128]{1,0:T(8,128)S(1)}, u32[]{:S(2)}, u32[]{:S(2)}) collective-permute-start(f32[200,128]{1,0:T(8,128)S(1)} %get-tuple-element.27), channel_id=1, source_target_pairs={{0,1},{1,0},{2,3},{3,2},{4,5},{5,4},{6,7},{7,6},{8,9},{9,8},{10,11... | collective-permute-start | bytes 307208 | tf_op jit(solution)/shard_map/ppermute | solution.py:362
  21.2 2.2 %collective-permute-start.7 = (f32[200,128]{1,0:T(8,128)S(1)}, f32[200,128]{1,0:T(8,128)S(1)}, u32[]{:S(2)}, u32[]{:S(2)}) collective-permute-start(f32[200,128]{1,0:T(8,128)S(1)} %get-tuple-element.28), channel_id=1, source_target_pairs={{0,16},{1,2},{2,1},{3,4},{4,3},{5,6},{6,5},{7,8},{8,7},{9,10},{10,... | collective-permute-start | bytes 307208 | tf_op jit(solution)/shard_map/ppermute | solution.py:362
  23.4 0.0 copy-done
  23.4 0.0 copy-done.1
  23.4 1.9 %slope_middle.1.slope = f32[336,256]{1,0:T(8,128)S(1)} custom-call(f32[2,512,128]{2,1,0:T(8,128)S(1)} %get-tuple-element.24.tiles, f32[2,144,128]{2,1,0:T(8,128)S(1)} %collective-permute-done.4.xe, f32[2,144,128]{2,1,0:T(8,128)S(1)} %collective-permute-done.5.xo, bf16[2560,256]{1,0:T(8,128)(2,1)S(1)} %copy-done.1, bf16[2560,256]{1,0:T(8,128)(2,1)S(1)} %copy-done), custom_call_target="tpu_custom_call" | custom-call | flops 1300000000 | bytes 31457280 | tf_op jit(solution)/shard_map/slope_middle/pallas_call | solution.py:436
  25.3 0.0 collective-permute-done.xe
  25.3 0.0 collective-permute-done.1.xo
  25.3 0.5 %columns.1 = (f32[376,128]{1,0:T(8,128)S(1)}, f32[376,128]{1,0:T(8,128)S(1)}) custom-call(f32[3,1024,128]{2,1,0:T(8,128)S(1)} %get-tuple-element.19.own, f32[3,200,128]{2,1,0:T(8,128)S(1)} %collective-permute-done.xe, f32[3,200,128]{2,1,0:T(8,128)S(1)} %collective-permute-done.1.xo), custom_call_target="tpu_custom_call" | custom-call | bytes 4194304 | tf_op jit(solution)/shard_map/columns/pallas_call | solution.py:445
  25.8 0.8 %collective-permute-start.2 = (f32[376,128]{1,0:T(8,128)S(1)}, f32[376,128]{1,0:T(8,128)S(1)}, u32[]{:S(2)}, u32[]{:S(2)}) collective-permute-start(f32[376,128]{1,0:T(8,128)S(1)} %get-tuple-element.22), channel_id=1, source_target_pairs={{0,1},{1,0},{2,3},{3,2},{4,5},{5,4},{6,7},{7,6},{8,9},{9,8},{10,11... | collective-permute-start | bytes 577544 | tf_op jit(solution)/shard_map/ppermute | solution.py:362
  26.6 1.4 %collective-permute-start.3 = (f32[376,128]{1,0:T(8,128)S(1)}, f32[376,128]{1,0:T(8,128)S(1)}, u32[]{:S(2)}, u32[]{:S(2)}) collective-permute-start(f32[376,128]{1,0:T(8,128)S(1)} %get-tuple-element.23), channel_id=1, source_target_pairs={{0,16},{1,2},{2,1},{3,4},{4,3},{5,6},{6,5},{7,8},{8,7},{9,10},{10,... | collective-permute-start | bytes 577544 | tf_op jit(solution)/shard_map/ppermute | solution.py:362
  28.0 0.0 collective-permute-done.6.ye
  28.0 0.0 collective-permute-done.7.yo
  28.0 3.5 %slope_sides.1 = (f32[336,256]{1,0:T(8,128)S(1)}, f32[336,256]{1,0:T(8,128)S(1)}) custom-call(f32[2,512,128]{2,1,0:T(8,128)S(1)} %get-tuple-element.24.tiles, f32[2,144,128]{2,1,0:T(8,128)S(1)} %collective-permute-done.4.xe, f32[2,144,128]{2,1,0:T(8,128)S(1)} %collective-permute-done.5.xo, f32[200,128]{1,0:T(8,128)S(1)} %collective-permute-done.6.ye, ...), custom_call_target="tpu_custom_call" | custom-call | flops 2600000000 | bytes 4194304 | tf_op jit(solution)/shard_map/slope_sides/pallas_call | solution.py:439
  31.5 1.3 %gradient_middle.1.middle = f32[256,256]{1,0:T(8,128)S(1)} custom-call(f32[3,1024,128]{2,1,0:T(8,128)S(1)} %get-tuple-element.19.own, f32[3,200,128]{2,1,0:T(8,128)S(1)} %collective-permute-done.xe, f32[3,200,128]{2,1,0:T(8,128)S(1)} %collective-permute-done.1.xo, f32[336,256]{1,0:T(8,128)S(1)} %get-tuple-element.29.left_slope, ...), custom_call_target="tpu_custom_call" | custom-call | flops 1000000000 | bytes 4194304 | tf_op jit(solution)/shard_map/gradient_middle/pallas_call | solution.py:448
  32.8 0.0 collective-permute-done.2.ye
  32.8 1.9 %collective-permute-done.3.yo = f32[376,128]{1,0:T(8,128)S(1)} collective-permute-done((f32[376,128]{1,0:T(8,128)S(1)}, f32[376,128]{1,0:T(8,128)S(1)}, u32[]{:S(2)}, u32[]{:S(2)}) %collective-permute-start.3) | collective-permute-done | bytes 192544 | tf_op jit(solution)/shard_map/ppermute | solution.py:362
  34.7 4.0 %gradient_sides.1 = f32[8,64,256]{2,1,0:T(8,128)} custom-call(f32[3,1024,128]{2,1,0:T(8,128)S(1)} %get-tuple-element.19.own, f32[3,200,128]{2,1,0:T(8,128)S(1)} %collective-permute-done.xe, f32[3,200,128]{2,1,0:T(8,128)S(1)} %collective-permute-done.1.xo, f32[376,128]{1,0:T(8,128)S(1)} %collective-permute-done.2.ye, ...), custom_call_target="tpu_custom_call" | custom-call | flops 2000000000 | bytes 4194304 | tf_op jit(solution)/shard_map/gradient_sides/pallas_call | solution.py:458
Async XLA Ops:
  1.9 21.5 %copy-start = (bf16[2560,256]{1,0:T(8,128)(2,1)S(1)}, bf16[2560,256]{1,0:T(8,128)(2,1)}, u32[]{:S(2)}) copy-start(bf16[2560,256]{1,0:T(8,128)(2,1)} %constant.5.clone.low_ref) | copy-start | bytes 3932164
  1.9 21.5 %copy-start.1 = (bf16[2560,256]{1,0:T(8,128)(2,1)S(1)}, bf16[2560,256]{1,0:T(8,128)(2,1)}, u32[]{:S(2)}) copy-start(bf16[2560,256]{1,0:T(8,128)(2,1)} %constant.4.clone.high_ref) | copy-start | bytes 3932164
  10.6 14.7 %collective-permute-start = (f32[3,200,128]{2,1,0:T(8,128)S(1)}, f32[3,200,128]{2,1,0:T(8,128)S(1)}, u32[]{:S(2)}, u32[]{:S(2)}) collective-permute-start(f32[3,200,128]{2,1,0:T(8,128)S(1)} %get-tuple-element.20), channel_id=1, source_target_pairs={{0,16},{1,17},{2,18},{3,19},{4,20},{5,21},{6,22},{7,23},{8,24},{9,... | collective-permute-start | bytes 921608 | tf_op jit(solution)/shard_map/ppermute | solution.py:362
  10.7 14.6 %collective-permute-start.1 = (f32[3,200,128]{2,1,0:T(8,128)S(1)}, f32[3,200,128]{2,1,0:T(8,128)S(1)}, u32[]{:S(2)}, u32[]{:S(2)}) collective-permute-start(f32[3,200,128]{2,1,0:T(8,128)S(1)} %get-tuple-element.21), channel_id=1, source_target_pairs={{0,1},{1,0},{2,3},{3,2},{4,5},{5,4},{6,7},{7,6},{8,9},{9,8},{10,11... | collective-permute-start | bytes 921608 | tf_op jit(solution)/shard_map/ppermute | solution.py:362
  12.3 2.0 %collective-permute-start.4 = (f32[2,144,128]{2,1,0:T(8,128)S(1)}, f32[2,144,128]{2,1,0:T(8,128)S(1)}, u32[]{:S(2)}, u32[]{:S(2)}) collective-permute-start(f32[2,144,128]{2,1,0:T(8,128)S(1)} %get-tuple-element.25), channel_id=1, source_target_pairs={{0,16},{1,17},{2,18},{3,19},{4,20},{5,21},{6,22},{7,23},{8,24},{9,... | collective-permute-start | bytes 442376 | tf_op jit(solution)/shard_map/ppermute | solution.py:362
  12.8 6.4 %collective-permute-start.5 = (f32[2,144,128]{2,1,0:T(8,128)S(1)}, f32[2,144,128]{2,1,0:T(8,128)S(1)}, u32[]{:S(2)}, u32[]{:S(2)}) collective-permute-start(f32[2,144,128]{2,1,0:T(8,128)S(1)} %get-tuple-element.26), channel_id=1, source_target_pairs={{0,1},{1,0},{2,3},{3,2},{4,5},{5,4},{6,7},{7,6},{8,9},{9,8},{10,11... | collective-permute-start | bytes 442376 | tf_op jit(solution)/shard_map/ppermute | solution.py:362
  19.6 8.4 %collective-permute-start.6 = (f32[200,128]{1,0:T(8,128)S(1)}, f32[200,128]{1,0:T(8,128)S(1)}, u32[]{:S(2)}, u32[]{:S(2)}) collective-permute-start(f32[200,128]{1,0:T(8,128)S(1)} %get-tuple-element.27), channel_id=1, source_target_pairs={{0,1},{1,0},{2,3},{3,2},{4,5},{5,4},{6,7},{7,6},{8,9},{9,8},{10,11... | collective-permute-start | bytes 307208 | tf_op jit(solution)/shard_map/ppermute | solution.py:362
  21.2 6.8 %collective-permute-start.7 = (f32[200,128]{1,0:T(8,128)S(1)}, f32[200,128]{1,0:T(8,128)S(1)}, u32[]{:S(2)}, u32[]{:S(2)}) collective-permute-start(f32[200,128]{1,0:T(8,128)S(1)} %get-tuple-element.28), channel_id=1, source_target_pairs={{0,16},{1,2},{2,1},{3,4},{4,3},{5,6},{6,5},{7,8},{8,7},{9,10},{10,... | collective-permute-start | bytes 307208 | tf_op jit(solution)/shard_map/ppermute | solution.py:362
  25.8 7.0 %collective-permute-start.2 = (f32[376,128]{1,0:T(8,128)S(1)}, f32[376,128]{1,0:T(8,128)S(1)}, u32[]{:S(2)}, u32[]{:S(2)}) collective-permute-start(f32[376,128]{1,0:T(8,128)S(1)} %get-tuple-element.22), channel_id=1, source_target_pairs={{0,1},{1,0},{2,3},{3,2},{4,5},{5,4},{6,7},{7,6},{8,9},{9,8},{10,11... | collective-permute-start | bytes 577544 | tf_op jit(solution)/shard_map/ppermute | solution.py:362
  26.6 8.1 %collective-permute-start.3 = (f32[376,128]{1,0:T(8,128)S(1)}, f32[376,128]{1,0:T(8,128)S(1)}, u32[]{:S(2)}, u32[]{:S(2)}) collective-permute-start(f32[376,128]{1,0:T(8,128)S(1)} %get-tuple-element.23), channel_id=1, source_target_pairs={{0,16},{1,2},{2,1},{3,4},{4,3},{5,6},{6,5},{7,8},{8,7},{9,10},{10,... | collective-permute-start | bytes 577544 | tf_op jit(solution)/shard_map/ppermute | solution.py:362
where the time goes:
time: 38.8 us; the launch traced here: 38.7 us
  Pallas kernels  22.1 us (57%)
  starting transfers between devices  9.74 us (25%)
  waiting for transfers between devices  6.73 us (17%)
    ppermute x8, starting transfers between devices, exchange(): arrived.append(lax.ppermute(value, ('gx', 'gy'), moves))  9.74 us
    pallas_call x1, Pallas kernels, body(): call(correlate_kernel, 'correlate', [ANY, ANY, SMEM], [whole_frame, side,...  8.67 us
    ppermute x8, waiting for transfers between devices, exchange(): arrived.append(lax.ppermute(value, ('gx', 'gy'), moves))  6.73 us
    pallas_call x1, Pallas kernels, body(): call(gradient_sides_kernel, 'gradient_sides', [VMEM] * 11, shaped(*densit...  3.98 us
    pallas_call x1, Pallas kernels, body(): call(slope_sides_kernel, 'slope_sides', [VMEM] * 7, [slope, slope], work(...  3.47 us
    pallas_call x1, Pallas kernels, body(): call(slope_middle_kernel, 'slope_middle', [VMEM] * 5, slope, work(DENSITY...  1.87 us
    pallas_call x1, Pallas kernels, body(): call(start_kernel, 'start', [ANY] * 4, [halo, halo, tile, shaped(SETTINGS...  1.87 us
    pallas_call x1, Pallas kernels, body(): call(gradient_middle_kernel, 'gradient_middle', [VMEM] * 8, shaped(ROWS /...  1.33 us
  transfers between devices with their start and end apart: 8, of which 2 were waited for; matrix products, arithmetic and copies ran while one was open for 0% of the time, Pallas kernels for 20%

commit v1 on v0

v1 whole, which is shorter than its diff:
```python
import jax
import jax.numpy as jnp
import ml_dtypes
import numpy as np
from jax import lax
from jax.experimental import pallas as pl
from jax.experimental.pallas import tpu as pltpu
from jax.sharding import PartitionSpec as P

RADIUS = 10
REACH = RADIUS - 1
TAPS = 2 * REACH + 1
BETA = 64.0
ETA = 0.5
LANES = 128
LAYERS = 8
QUAD = 4
PIECE = 64
SPAN = PIECE - 2 * REACH
LAGS = 6
ROWS, COLS = 64, 256
GROUP_ROWS, GROUP_COLS = 96, 384
ROW_SLACK, COL_SLACK = 16, 64
FRAME_ROWS = GROUP_ROWS + 2 * ROW_SLACK
SIDE = ROW_SLACK + REACH
FIRST = ROW_SLACK - REACH
NEED = ROWS + 2 * REACH
HALO = 2 * REACH
GROUPS = LANES // HALO
GROUPED = -(-(ROWS + 2 * HALO) // GROUPS)
INNER = (SIDE + FIRST, ROWS)
HALF = (INNER[1] - INNER[0]) // 2
WINDOWS = 6
STARTS = [SPAN * w - HALO for w in range(WINDOWS)]
MIDDLE_SLOPES = (1, 2, 3, 4)
MIDDLE = (2, 3)
SLOPE_ROWS = 176
DENSITY_QUADS = SLOPE_ROWS // LAYERS + LAGS - 1
GRADIENT_ROWS = ROWS // QUAD * LAYERS
GRADIENT_QUADS = ROWS // QUAD + LAGS - 1
CHUNK = GROUP_ROWS // 2
F32 = jnp.float32
BF16 = jnp.bfloat16


def cone_blocks():
    offsets = np.arange(-RADIUS, RADIUS + 1).astype(np.float64)
    cone = np.maximum(1.0 - np.sqrt(offsets[:, None] ** 2 + offsets[None, :] ** 2) / RADIUS, 0.0)
    cone = (cone / cone.sum())[1:-1, 1:-1]
    blocks = np.zeros((LAGS, QUAD, PIECE, QUAD, PIECE))
    lanes = np.arange(2 * REACH, PIECE)
    for lag in range(LAGS):
        for source in range(QUAD):
            for target in range(QUAD):
                a = QUAD * lag + source - target
                if 0 <= a < TAPS:
                    for b in range(TAPS):
                        blocks[lag, source, lanes + b - 2 * REACH, target, lanes] = cone[a, b]
    blocks = blocks.reshape(LAGS * QUAD * PIECE, QUAD * PIECE)
    high = blocks.astype(ml_dtypes.bfloat16)
    low = (blocks - high.astype(np.float64)).astype(ml_dtypes.bfloat16)
    return high, low


def lane_of(rows):
    return lax.broadcasted_iota(jnp.int32, (rows, LANES), 1)


def turn(value, shift):
    return pltpu.roll(value, shift % LANES, 1)


def place():
    i, j = lax.axis_index("gx"), lax.axis_index("gy")
    return i, j, lax.rem(i, 2), lax.rem(j, 2)


def sides_of():
    i, j = lax.axis_index("gx"), lax.axis_index("gy")
    return i > 0, i < lax.axis_size("gx") - 1, j > 0, j < lax.axis_size("gy") - 1


def chosen(parity, first, second):
    return jnp.where(parity == 0, first, second)


def row_at(e):
    return slice(e * LAYERS, (e + 1) * LAYERS)


def half_at(e):
    return row_at(e // QUAD), slice((e % QUAD) * PIECE, (e % QUAD) * PIECE + LANES)


def piece_of(tiles, start):
    k, first = divmod(start, LANES)
    value = tiles[k]
    if first > LANES - PIECE:
        value = jnp.where(lane_of(LAYERS) >= first, value, tiles[k + 1])
    return turn(value, -first), turn(value, PIECE - first)


def correlate_kernel(forward, adjoint, weights, rows, cols, frame, xe, xo, fields, w_smem, r_smem, c_smem, sems, small):
    i, j, pi, pj = place()
    scalars = [
        pltpu.make_async_copy(source, target, small.at[n])
        for n, (source, target) in enumerate(((weights, w_smem), (rows, r_smem), (cols, c_smem)))
    ]

    def copies(n):
        at = pl.ds(pl.multiple_of(lax.rem(n, 2) * CHUNK, CHUNK), CHUNK)
        return [
            pltpu.make_async_copy(source.at[:, :, :, lax.div(n, 2), at], fields.at[k, :, :, :, n], sems.at[k, n])
            for k, source in enumerate((forward, adjoint))
        ]

    for copy in scalars:
        copy.start()
    for n in range(2 * LAYERS):
        for copy in copies(jnp.int32(n)):
            copy.start()
    frame[...] = jnp.zeros_like(frame)
    for copy in scalars:
        copy.wait()
    down = r_smem[i] - i * ROWS + ROW_SLACK
    across = c_smem[j] - j * COLS + COL_SLACK
    span_rows = r_smem[i + 1] - r_smem[i]
    span_cols = c_smem[j + 1] - c_smem[j]
    lane = lane_of(16)
    row = lax.broadcasted_iota(jnp.int32, (16, LANES), 0)
    turned = lax.rem(across, LANES)

    @pl.loop(0, 2 * LAYERS)
    def _(n):
        for copy in copies(n):
            copy.wait()
        z, top = lax.div(n, 2), lax.rem(n, 2) * CHUNK
        for r in range(0, CHUNK, 16):
            before = jnp.zeros((16, LANES), F32)
            for k in range(3):
                at = (n, slice(r, r + 16), slice(LANES * k, LANES * (k + 1)))
                total = None
                for w in range(3):
                    real = imag = None
                    for c in range(3):
                        fr = fields[(0, 0, w, c) + at].astype(F32)
                        fi = fields[(0, 1, w, c) + at].astype(F32)
                        ar = fields[(1, 0, w, c) + at].astype(F32)
                        ai = fields[(1, 1, w, c) + at].astype(F32)
                        re = fr * ar - fi * ai
                        im = fr * ai + fi * ar
                        real = re if real is None else real + re
                        imag = im if imag is None else imag + im
                    term = w_smem[0, w] * real - w_smem[1, w] * imag
                    total = term if total is None else total + term
                inside = (row < span_rows - top - r) & (lane < span_cols - LANES * k)
                total = pltpu.roll(jnp.where(inside, total, 0.0), turned, 1)
                value = jnp.where(lane >= across, total, before)
                before = total
                frame[k, pl.ds((top + r + down) * LAYERS + z, 16, stride=LAYERS), :] = value

    for parity, out in ((0, xe), (1, xo)):
        start = pl.multiple_of(jnp.where(pi == parity, ROWS + FIRST, 0) * LAYERS, 8)
        out[...] = frame[:, pl.ds(start, SIDE * LAYERS), :]


def density_rows_kernel(flat, xe, xo, tiles, sems):
    i, j, pi, pj = place()
    copies = [pltpu.make_async_copy(flat.at[:, LANES * k : LANES * (k + 1)], tiles.at[k], sems.at[k]) for k in range(2)]
    for copy in copies:
        copy.start()
    for copy in copies:
        copy.wait()
    for parity, out in ((0, xe), (1, xo)):
        start = jnp.where(pi == parity, ROWS - HALO, 0)
        for r in range(HALO):
            for k in range(2):
                out[k, row_at(r), :] = tiles[k, pl.ds(start + r, LAYERS, stride=ROWS), :]


def density_row(tiles, xe, xo, e, k):
    i, j, pi, pj = place()
    has_up, has_down, has_left, has_right = sides_of()
    if e >= ROWS + 2 * HALO:
        return jnp.zeros((LAYERS, LANES), F32)
    if HALO <= e < HALO + ROWS:
        return tiles[k, pl.ds(e - HALO, LAYERS, stride=ROWS), :]
    at = (k, row_at(e % (HALO + ROWS)))
    if e < HALO:
        return jnp.where(has_up, chosen(pi, xo[at], xe[at]), 0.0)
    return jnp.where(has_down, chosen(pi, xe[at], xo[at]), 0.0)


def side_pack(frame, out, first_row, right, blocks, nines, count):
    tile = jnp.where(right, 2, 0)
    size = blocks[0][1] * LAYERS
    upper = lane_of(size)
    first, second = [frame[tile, at * LAYERS : at * LAYERS + size, :] for at, _ in blocks]
    swing = jnp.where(right, 0, 64)
    out[first_row : first_row + size, :] = jnp.where(
        upper >= 64, pltpu.roll(first, swing, 1), pltpu.roll(second, 64 - swing, 1)
    )
    lower = lane_of(count * LAYERS)
    packed = None
    base = jnp.where(right, LANES - 55, 64)
    for g, (at, _) in enumerate(nines):
        value = frame[tile, at * LAYERS : (at + count) * LAYERS, :]
        value = pltpu.roll(value, lax.rem(base + REACH * g, LANES), 1)
        packed = value if g == 0 else jnp.where(lower >= REACH * g, value, packed)
    out[first_row + size : first_row + size + count * LAYERS, :] = packed


def side_unpack(frame, packed, first_row, tile, valid, blocks, nines, count):
    from_left = tile == 0
    size = blocks[0][1] * LAYERS
    lane = lane_of(size)
    keep = ((lane >= 64) if from_left else (lane < 64)) & valid
    value = packed(first_row, size)
    for h, (at, _) in enumerate(blocks):
        shown = turn(value, 64) if (h == 0) != from_left else value
        frame[tile, at * LAYERS : at * LAYERS + size, :] += jnp.where(keep, shown, 0.0)
    value = packed(first_row + size, count * LAYERS)
    start = 55 if from_left else 64
    lane = lane_of(count * LAYERS)
    keep = (lane >= start) & (lane < start + REACH) & valid
    for g, (at, rows) in enumerate(nines):
        shown = jnp.where(keep, turn(value, start - REACH * g), 0.0)
        frame[tile, at * LAYERS : (at + rows) * LAYERS, :] += shown[0 : rows * LAYERS, :]


def split_rows(first, end, count):
    return [(at, min(count, end - at)) for at in range(first, end, count)]


INNER_SIDE = (((INNER[0], HALF), (INNER[0] + HALF, HALF)), split_rows(*INNER, 3), 3)
OUTER_SIDE = (((FIRST, SIDE), (ROWS, SIDE)), split_rows(FIRST, FIRST + SIDE, 4) + split_rows(ROWS, ROWS + SIDE, 4), 4)
DENSITY_PART = GROUPED * LAYERS


def side_size(side):
    return (side[0][0][1] + side[2]) * LAYERS


def first_columns_kernel(tiles, xe, xo, own, ye, yo):
    i, j, pi, pj = place()
    lane = lane_of(LAYERS)
    for r in range(GROUPED):
        left = right = None
        for g in range(GROUPS):
            a = turn(density_row(tiles, xe, xo, g * GROUPED + r, 0), HALO * g)
            b = turn(density_row(tiles, xe, xo, g * GROUPED + r, 1), HALO * g + HALO)
            left = a if g == 0 else jnp.where(lane >= HALO * g, a, left)
            right = b if g == 0 else jnp.where(lane >= HALO * g, b, right)
        ye[row_at(r), :] = chosen(pj, right, left)
        yo[row_at(r), :] = chosen(pj, left, right)
    for parity, out in ((0, ye), (1, yo)):
        side_pack(own, out, DENSITY_PART, pj == parity, *INNER_SIDE)


def banded(windows, copies, count, rows, high_ref, low_ref):
    size = rows + LAYERS * (LAGS - 2)
    for w in range(count):
        for shift in range(2):
            for r in range(0, size, 16):
                value = windows[w, r + shift * LAYERS : r + shift * LAYERS + 16, :]
                high = value.astype(BF16)
                copies[w, shift, 0, r : r + 16, :] = high
                copies[w, shift, 1, r : r + 16, :] = (value - high.astype(F32)).astype(BF16)

    def part(kind):
        return jnp.concatenate(
            [
                jnp.concatenate(
                    [copies[w, lag % 2, kind, 16 * (lag // 2) : 16 * (lag // 2) + rows, :] for lag in range(LAGS)],
                    axis=1,
                )
                for w in range(count)
            ],
            axis=0,
        )

    high = part(0)
    out = jnp.dot(part(1), high_ref[...], preferred_element_type=F32)
    out += jnp.dot(high, low_ref[...], preferred_element_type=F32)
    return out + jnp.dot(high, high_ref[...], preferred_element_type=F32)


def slope_of(filtered):
    e = jnp.exp(-2.0 * BETA * jnp.abs(filtered - ETA))
    scale = 4.0 * BETA / (np.tanh(BETA * ETA) + np.tanh(BETA * (1.0 - ETA)))
    return np.float32(scale) * e / ((1.0 + e) * (1.0 + e))


def store_slope(value, out, count):
    for w in range(count):
        out[w] = slope_of(value[w * SLOPE_ROWS : (w + 1) * SLOPE_ROWS, :])


def slope_middle_kernel(tiles, xe, xo, high_ref, low_ref, slope, windows, copies):
    lower = lane_of(LAYERS) < PIECE
    for e in range(0, QUAD * DENSITY_QUADS, 2):
        even, odd = [[density_row(tiles, xe, xo, e + h, k) for k in range(2)] for h in range(2)]
        for n, w in enumerate(MIDDLE_SLOPES):
            windows[(n,) + half_at(e)] = jnp.where(
                lower, piece_of(even, STARTS[w])[0], piece_of(odd, STARTS[w])[1]
            )
    count = len(MIDDLE_SLOPES)
    store_slope(banded(windows, copies, count, SLOPE_ROWS, high_ref, low_ref), slope, count)


def slope_sides_kernel(tiles, xe, xo, ye, yo, high_ref, low_ref, slope, windows, copies):
    i, j, pi, pj = place()
    has_up, has_down, has_left, has_right = sides_of()
    lane = lane_of(LAYERS)
    lower = lane < PIECE
    within = jnp.where(lower, lane, lane - PIECE)
    own_left, own_right = within >= HALO, within < COLS - STARTS[-1]
    edge = within < COLS - STARTS[-1] + HALO
    for e in range(0, QUAD * DENSITY_QUADS, 2):
        lefts, rights = [], []
        for h in range(2):
            g, r = divmod(min(e + h, GROUPS * GROUPED - 1), GROUPED)
            at = row_at(r)
            left = jnp.where(has_left, chosen(pj, yo[at, :], ye[at, :]), 0.0)
            right = jnp.where(has_right, chosen(pj, ye[at, :], yo[at, :]), 0.0)
            left = turn(left, PIECE * h - HALO * g)
            right = turn(right, PIECE * h + COLS - STARTS[-1] - HALO * g)
            t0, t1 = [density_row(tiles, xe, xo, e + h, k) for k in range(2)]
            lefts.append(jnp.where(own_left, turn(t0, PIECE * h - STARTS[0]), left))
            rights.append(
                jnp.where(own_right, turn(t1, PIECE * h + LANES - STARTS[-1]), jnp.where(edge, right, 0.0))
            )
        windows[(0,) + half_at(e)] = jnp.where(lower, *lefts)
        windows[(1,) + half_at(e)] = jnp.where(lower, *rights)
    store_slope(banded(windows, copies, 2, SLOPE_ROWS, high_ref, low_ref), slope, 2)


def add_rows(frame, xe, xo, tiles):
    i, j, pi, pj = place()
    has_up, has_down, has_left, has_right = sides_of()
    size = SIDE * LAYERS
    for k in tiles:
        frame[k, FIRST * LAYERS : FIRST * LAYERS + size, :] += jnp.where(has_up, chosen(pi, xo[k], xe[k]), 0.0)
        frame[k, ROWS * LAYERS : ROWS * LAYERS + size, :] += jnp.where(has_down, chosen(pi, xe[k], xo[k]), 0.0)


def columns_kernel(own, xe, xo, ye, yo, frame):
    i, j, pi, pj = place()
    for k in (0, 2):
        frame[k] = own[k, 0 : GROUP_ROWS * LAYERS, :]
    add_rows(frame, xe, xo, (0, 2))
    for parity, out in ((0, ye), (1, yo)):
        side_pack(frame, out, 0, pj == parity, *OUTER_SIDE)


def add_columns(frame, ye, yo, first_row, side):
    i, j, pi, pj = place()
    has_up, has_down, has_left, has_right = sides_of()

    def pick(first, second):
        return lambda at, count: chosen(pj, first[at : at + count, :], second[at : at + count, :])

    side_unpack(frame, pick(yo, ye), first_row, 0, has_left, *side)
    side_unpack(frame, pick(ye, yo), first_row, 2, has_right, *side)


def weigh(frame, windows, n, w, slope, before):
    lane = lane_of(LAYERS)
    lower = lane < PIECE
    own = jnp.where(lower, lane, lane - PIECE) >= 2 * REACH
    for e in range(0, QUAD * GRADIENT_QUADS, 2):
        at = half_at(e)
        even, odd = [[frame[k, row_at(FIRST + e + h), :] for k in range(3)] for h in range(2)]
        start = STARTS[w] - REACH + COL_SLACK
        factor = slope[at] if before is None else jnp.where(own, slope[at], turn(before[at], -SPAN))
        windows[(n,) + at] = jnp.where(lower, piece_of(even, start)[0], piece_of(odd, start)[1]) * factor


def gradient_middle_kernel(own, xe, xo, ye, yo, slope, high_ref, low_ref, out, frame, windows, copies):
    frame[...] = own[:, 0 : GROUP_ROWS * LAYERS, :]
    add_rows(frame, xe, xo, range(3))
    for n, w in enumerate(MIDDLE):
        weigh(frame, windows, n, w, slope.at[w - 1], slope.at[w - 2])
    out[...] = banded(windows, copies, len(MIDDLE), GRADIENT_ROWS, high_ref, low_ref)
    add_columns(frame, ye, yo, DENSITY_PART, INNER_SIDE)


def gradient_sides_kernel(given, ye, yo, slope, outer, middle, high_ref, low_ref, out, frame, windows, copies, result):
    frame[...] = given[...]
    add_columns(frame, ye, yo, 0, OUTER_SIDE)
    weigh(frame, windows, 0, 0, outer.at[0], None)
    weigh(frame, windows, 1, 1, slope.at[0], outer.at[0])
    weigh(frame, windows, 2, 4, slope.at[3], slope.at[2])
    weigh(frame, windows, 3, 5, outer.at[1], slope.at[3])
    result[...] = banded(windows, copies, 4, GRADIENT_ROWS, high_ref, low_ref)
    lane = lane_of(LAYERS)
    places = ((result, 0), (result, 1), (middle, 0), (middle, 1), (result, 2), (result, 3))
    for e in range(ROWS):
        rows, lanes = half_at(e - e % 2)
        pieces = []
        for w, (source, n) in enumerate(places):
            at = slice(rows.start + n * GRADIENT_ROWS, rows.stop + n * GRADIENT_ROWS)
            pieces.append(turn(source[at, lanes], STARTS[w] - 2 * REACH - PIECE * (e % 2)))
        for k in range(2):
            value = None
            for w, piece in enumerate(pieces):
                first = STARTS[w] - LANES * k
                if first < LANES and first + SPAN > 0:
                    value = piece if value is None else jnp.where(lane >= first, piece, value)
            frame[k, row_at(e), :] = value
    for z in range(LAYERS):
        for k in range(2):
            out[z, :, LANES * k : LANES * (k + 1)] = frame[k, pl.ds(z, ROWS, stride=LAYERS), :]


def partner(index, count, parity):
    other = index ^ 1 if parity == 0 else ((index - 1) ^ 1) + 1
    return other if 0 <= other < count else None


def exchange(pair, axis):
    nx, ny = lax.axis_size("gx"), lax.axis_size("gy")
    arrived = []
    for parity, value in enumerate(pair):
        moves = []
        for i in range(nx):
            for j in range(ny):
                to = (partner(i, nx, parity), j) if axis == "gx" else (i, partner(j, ny, parity))
                if None in to:
                    to = (i, j ^ 1) if axis == "gx" else (i ^ 1, j)
                moves.append((i * ny + j, to[0] * ny + to[1]))
        arrived.append(lax.ppermute(value, ("gx", "gy"), moves))
    return arrived


ANY = pl.BlockSpec(memory_space=pl.ANY)
VMEM = pl.BlockSpec(memory_space=pltpu.VMEM)


def shaped(*shape):
    return jax.ShapeDtypeStruct(shape, F32)


def call(kernel, name, ins, outs, scratch, mib, flops, moved):
    return pl.pallas_call(
        kernel,
        out_shape=outs,
        in_specs=ins,
        out_specs=jax.tree.map(lambda s: VMEM, outs),
        scratch_shapes=scratch,
        compiler_params=pltpu.CompilerParams(vmem_limit_bytes=mib << 20),
        cost_estimate=pl.CostEstimate(flops=int(flops), bytes_accessed=int(moved * (1 << 20)), transcendentals=0),
        name=name,
    )


def body(forward, adjoint, weights, density, row_edges, column_edges):
    high, low = (jnp.asarray(m) for m in cone_blocks())
    forward, adjoint, flat, weights, row_edges, column_edges = [
        pltpu.with_memory_space_constraint(x, pltpu.HBM)
        for x in (forward, adjoint, density.reshape(LAYERS * ROWS, COLS), weights, row_edges, column_edges)
    ]
    halo = shaped(2, HALO * LAYERS, LANES)
    tile = shaped(2, LAYERS * ROWS, LANES)
    whole_frame = shaped(3, FRAME_ROWS * LAYERS, LANES)
    *halo_rows, tiles = call(
        density_rows_kernel, "density_rows", [ANY], [halo, halo, tile], [pltpu.SemaphoreType.DMA((2,))], 2, 0, 1
    )(flat)
    halo_rows = exchange(halo_rows, "gx")

    side = shaped(3, SIDE * LAYERS, LANES)
    frame, *own_rows = call(
        correlate_kernel,
        "correlate",
        [ANY] * 5,
        [whole_frame, side, side],
        [
            pltpu.VMEM((2, 2, 3, 3, 2 * LAYERS, CHUNK, GROUP_COLS), BF16),
            pltpu.SMEM((2, 3), F32),
            pltpu.SMEM(row_edges.shape, jnp.int32),
            pltpu.SMEM(column_edges.shape, jnp.int32),
            pltpu.SemaphoreType.DMA((2, 2 * LAYERS)),
            pltpu.SemaphoreType.DMA((3,)),
        ],
        28,
        0,
        24,
    )(forward, adjoint, weights, row_edges, column_edges)
    own_rows = exchange(own_rows, "gx")

    column = shaped(DENSITY_PART + side_size(INNER_SIDE), LANES)
    columns = call(first_columns_kernel, "first_columns", [VMEM] * 4, [column, column], [], 2, 0, 30)(
        tiles, *halo_rows, frame
    )
    columns = exchange(columns, "gy")

    def work(count, quads, rows):
        return [
            pltpu.VMEM((count, quads * LAYERS, QUAD * PIECE), F32),
            pltpu.VMEM((count, 2, 2, rows + LAYERS * (LAGS - 2), QUAD * PIECE), BF16),
        ]

    middle_slope = call(
        slope_middle_kernel,
        "slope_middle",
        [VMEM] * 5,
        shaped(len(MIDDLE_SLOPES), SLOPE_ROWS, QUAD * PIECE),
        work(len(MIDDLE_SLOPES), DENSITY_QUADS, SLOPE_ROWS),
        12,
        1e11,
        300,
    )(tiles, *halo_rows, high, low)
    outer_slope = call(
        slope_sides_kernel,
        "slope_sides",
        [VMEM] * 7,
        shaped(2, SLOPE_ROWS, QUAD * PIECE),
        work(2, DENSITY_QUADS, SLOPE_ROWS),
        8,
        2.6e9,
        4,
    )(tiles, *halo_rows, *columns, high, low)

    own_frame = pltpu.VMEM((3, GROUP_ROWS * LAYERS, LANES), F32)
    packed = shaped(side_size(OUTER_SIDE), LANES)
    own_columns = call(columns_kernel, "columns", [VMEM] * 3, [packed, packed], [own_frame], 4, 0, 4)(frame, *own_rows)
    own_columns = exchange(own_columns, "gy")

    middle, frame = call(
        gradient_middle_kernel,
        "gradient_middle",
        [VMEM] * 8,
        [shaped(len(MIDDLE) * GRADIENT_ROWS, QUAD * PIECE), shaped(3, GROUP_ROWS * LAYERS, LANES)],
        work(len(MIDDLE), GRADIENT_QUADS, GRADIENT_ROWS),
        8,
        1e9,
        4,
    )(frame, *own_rows, *columns, middle_slope, high, low)
    return call(
        gradient_sides_kernel,
        "gradient_sides",
        [VMEM] * 8,
        shaped(*density.shape),
        [own_frame] + work(4, GRADIENT_QUADS, GRADIENT_ROWS) + [pltpu.VMEM((4 * GRADIENT_ROWS, QUAD * PIECE), F32)],
        12,
        2e9,
        4,
    )(frame, *own_columns, middle_slope, outer_slope, middle, high, low)


def solution(mesh):
    placed = (
        P(None, None, None, None, "gx", "gy"),
        P(None, None, None, None, "gx", "gy"),
        P(),
        P(None, "gx", "gy"),
        P(),
        P(),
    )
    return jax.shard_map(body, mesh=mesh, in_specs=placed, out_specs=P(None, "gx", "gy"), check_vma=False)
```

time: 38.8 us -> 31.9 us (0.82)
  waiting for transfers between devices: 6.73 us -> 2.52 us
  Pallas kernels: 22.1 us -> 18 us
  starting transfers between devices: 9.74 us -> 11.2 us
    ppermute x8, waiting for transfers between devices: 6.73 us -> 2.52 us  [exchange(): arrived.append(lax.ppermute(value, ('gx', 'gy'), moves))]
    pallas_call x7, Pallas kernels: 21.6 us -> 17.6 us  [the longest x1 7.85 us: body(): call(correlate_kernel, 'correlate', [ANY] * 5, [whole_frame, side, side],...]
    ppermute x8, starting transfers between devices: 9.74 us -> 11.2 us  [exchange(): arrived.append(lax.ppermute(value, ('gx', 'gy'), moves))]
  transfers between devices with their start and end apart: 8 -> 8, of which waited for: 2 -> 2; matrix products, arithmetic and copies ran while one was open for 0% -> 0% of each run, Pallas kernels for 20% -> 43%
where the time goes in v1:
time: 31.9 us; the launch traced here: 31.8 us
  Pallas kernels  18 us (56%)
  starting transfers between devices  11.2 us (35%)
  waiting for transfers between devices  2.52 us (8%)
    ppermute x8, starting transfers between devices, exchange(): arrived.append(lax.ppermute(value, ('gx', 'gy'), moves))  11.2 us
    pallas_call x1, Pallas kernels, body(): call(correlate_kernel, 'correlate', [ANY] * 5, [whole_frame, side, side],...  7.85 us
    pallas_call x1, Pallas kernels, body(): call(gradient_sides_kernel, 'gradient_sides', [VMEM] * 8, shaped(*density...  3.06 us
    ppermute x8, waiting for transfers between devices, exchange(): arrived.append(lax.ppermute(value, ('gx', 'gy'), moves))  2.52 us
    pallas_call x1, Pallas kernels, body(): call(slope_middle_kernel, 'slope_middle', [VMEM] * 5, shaped(len(MIDDLE_S...  2.4 us
    pallas_call x1, Pallas kernels, body(): call(slope_sides_kernel, 'slope_sides', [VMEM] * 7, shaped(2, SLOPE_ROWS,...  1.48 us
    pallas_call x1, Pallas kernels, body(): call(density_rows_kernel, 'density_rows', [ANY], [halo, halo, tile], [plt...  1.22 us
    pallas_call x1, Pallas kernels, body(): call(gradient_middle_kernel, 'gradient_middle', [VMEM] * 8, [shaped(len(M...  1.08 us
  transfers between devices with their start and end apart: 8, of which 2 were waited for; matrix products, arithmetic and copies ran while one was open for 0% of the time, Pallas kernels for 43%

profile of v1, /device:TPU:2, one launch (start us, length us, event | category | flops | bytes accessed | tf_op | source)
XLA Modules:
  0.0 31.8 jit_solution(15172061005347152117)
XLA Ops:
  0.0 1.2 %density_rows.1 = (f32[2,144,128]{2,1,0:T(8,128)S(1)}, f32[2,144,128]{2,1,0:T(8,128)S(1)}, f32[2,512,128]{2,1,0:T(8,128)S(1)}) custom-call(f32[512,256]{1,0:T(8,128)} %bitcast.1), custom_call_target="tpu_custom_call" | custom-call | bytes 1048576 | tf_op jit(solution)/shard_map/density_rows/pallas_call | solution.py:466
  1.2 0.1 collective-permute-start.2
  1.3 0.0 copy-start
  1.3 0.0 copy-start.1
  1.3 1.7 %collective-permute-start.3 = (f32[2,144,128]{2,1,0:T(8,128)S(1)}, f32[2,144,128]{2,1,0:T(8,128)S(1)}, u32[]{:S(2)}, u32[]{:S(2)}) collective-permute-start(f32[2,144,128]{2,1,0:T(8,128)S(1)} %get-tuple-element.22), channel_id=1, source_target_pairs={{0,1},{1,0},{2,3},{3,2},{4,5},{5,4},{6,7},{7,6},{8,9},{9,8},{10,11... | collective-permute-start | bytes 442376 | tf_op jit(solution)/shard_map/ppermute | solution.py:432
  3.0 7.9 %correlate.1 = (f32[3,1024,128]{2,1,0:T(8,128)S(1)}, f32[3,200,128]{2,1,0:T(8,128)S(1)}, f32[3,200,128]{2,1,0:T(8,128)S(1)}) custom-call(bf16[2,3,3,8,96,384]{5,4,3,2,1,0:T(8,128)(2,1)} %forward.1, bf16[2,3,3,8,96,384]{5,4,3,2,1,0:T(8,128)(2,1)} %adjoint.1, f32[2,3]{1,0:T(2,128)} %weights.1, s32[9]{0:T(128)} %rows.1, s32[17]{0:T(128)} %cols.1), custom_call_target="tpu_custom_call" | custom-call | bytes 25165824 | tf_op jit(solution)/shard_map/correlate/pallas_call | solution.py:472
  10.9 0.5 %collective-permute-start = (f32[3,200,128]{2,1,0:T(8,128)S(1)}, f32[3,200,128]{2,1,0:T(8,128)S(1)}, u32[]{:S(2)}, u32[]{:S(2)}) collective-permute-start(f32[3,200,128]{2,1,0:T(8,128)S(1)} %get-tuple-element.18), channel_id=1, source_target_pairs={{0,16},{1,17},{2,18},{3,19},{4,20},{5,21},{6,22},{7,23},{8,24},{9,... | collective-permute-start | bytes 921608 | tf_op jit(solution)/shard_map/ppermute | solution.py:432
  11.4 1.6 %collective-permute-start.1 = (f32[3,200,128]{2,1,0:T(8,128)S(1)}, f32[3,200,128]{2,1,0:T(8,128)S(1)}, u32[]{:S(2)}, u32[]{:S(2)}) collective-permute-start(f32[3,200,128]{2,1,0:T(8,128)S(1)} %get-tuple-element.19), channel_id=1, source_target_pairs={{0,1},{1,0},{2,3},{3,2},{4,5},{5,4},{6,7},{7,6},{8,9},{9,8},{10,11... | collective-permute-start | bytes 921608 | tf_op jit(solution)/shard_map/ppermute | solution.py:432
  13.0 0.0 collective-permute-done.2.xe
  13.0 0.0 collective-permute-done.3.xo
  13.0 0.5 %first_columns.1 = (f32[272,128]{1,0:T(8,128)S(1)}, f32[272,128]{1,0:T(8,128)S(1)}) custom-call(f32[2,512,128]{2,1,0:T(8,128)S(1)} %get-tuple-element.20.tiles, f32[2,144,128]{2,1,0:T(8,128)S(1)} %collective-permute-done.2.xe, f32[2,144,128]{2,1,0:T(8,128)S(1)} %collective-permute-done.3.xo, f32[3,1024,128]{2,1,0:T(8,128)S(1)} %get-tuple-element.17.own), custom_call_target="tpu_custom_call" | custom-call | bytes 31457280 | tf_op jit(solution)/shard_map/first_columns/pallas_call | solution.py:492
  13.5 0.5 %collective-permute-start.4 = (f32[272,128]{1,0:T(8,128)S(1)}, f32[272,128]{1,0:T(8,128)S(1)}, u32[]{:S(2)}, u32[]{:S(2)}) collective-permute-start(f32[272,128]{1,0:T(8,128)S(1)} %get-tuple-element.23), channel_id=1, source_target_pairs={{0,1},{1,0},{2,3},{3,2},{4,5},{5,4},{6,7},{7,6},{8,9},{9,8},{10,11... | collective-permute-start | bytes 417800 | tf_op jit(solution)/shard_map/ppermute | solution.py:432
  14.0 3.0 %collective-permute-start.5 = (f32[272,128]{1,0:T(8,128)S(1)}, f32[272,128]{1,0:T(8,128)S(1)}, u32[]{:S(2)}, u32[]{:S(2)}) collective-permute-start(f32[272,128]{1,0:T(8,128)S(1)} %get-tuple-element.24), channel_id=1, source_target_pairs={{0,16},{1,2},{2,1},{3,4},{4,3},{5,6},{6,5},{7,8},{8,7},{9,10},{10,... | collective-permute-start | bytes 417800 | tf_op jit(solution)/shard_map/ppermute | solution.py:432
  17.0 0.0 copy-done
  17.0 0.0 copy-done.1
  17.0 2.4 %slope_middle.1.slope = f32[4,176,256]{2,1,0:T(8,128)S(1)} custom-call(f32[2,512,128]{2,1,0:T(8,128)S(1)} %get-tuple-element.20.tiles, f32[2,144,128]{2,1,0:T(8,128)S(1)} %collective-permute-done.2.xe, f32[2,144,128]{2,1,0:T(8,128)S(1)} %collective-permute-done.3.xo, bf16[1536,256]{1,0:T(8,128)(2,1)S(1)} %copy-done, bf16[1536,256]{1,0:T(8,128)(2,1)S(1)} %copy-done.1), custom_call_target="tpu_custom_call" | custom-call | flops 99999997952 | bytes 314572800 | tf_op jit(solution)/shard_map/slope_middle/pallas_call | solution.py:503
  19.4 0.0 collective-permute-done.xe
  19.4 0.3 collective-permute-done.1.xo
  19.7 0.4 %columns.1 = (f32[232,128]{1,0:T(8,128)S(1)}, f32[232,128]{1,0:T(8,128)S(1)}) custom-call(f32[3,1024,128]{2,1,0:T(8,128)S(1)} %get-tuple-element.17.own, f32[3,200,128]{2,1,0:T(8,128)S(1)} %collective-permute-done.xe, f32[3,200,128]{2,1,0:T(8,128)S(1)} %collective-permute-done.1.xo), custom_call_target="tpu_custom_call" | custom-call | bytes 4194304 | tf_op jit(solution)/shard_map/columns/pallas_call | solution.py:526
  20.1 1.7 %collective-permute-start.6 = (f32[232,128]{1,0:T(8,128)S(1)}, f32[232,128]{1,0:T(8,128)S(1)}, u32[]{:S(2)}, u32[]{:S(2)}) collective-permute-start(f32[232,128]{1,0:T(8,128)S(1)} %get-tuple-element.26), channel_id=1, source_target_pairs={{0,1},{1,0},{2,3},{3,2},{4,5},{5,4},{6,7},{7,6},{8,9},{9,8},{10,11... | collective-permute-start | bytes 356360 | tf_op jit(solution)/shard_map/ppermute | solution.py:432
  21.8 2.2 %collective-permute-start.7 = (f32[232,128]{1,0:T(8,128)S(1)}, f32[232,128]{1,0:T(8,128)S(1)}, u32[]{:S(2)}, u32[]{:S(2)}) collective-permute-start(f32[232,128]{1,0:T(8,128)S(1)} %get-tuple-element.27), channel_id=1, source_target_pairs={{0,16},{1,2},{2,1},{3,4},{4,3},{5,6},{6,5},{7,8},{8,7},{9,10},{10,... | collective-permute-start | bytes 356360 | tf_op jit(solution)/shard_map/ppermute | solution.py:432
  23.9 0.0 collective-permute-done.4.ye
  23.9 0.0 collective-permute-done.5.yo
  23.9 1.5 %slope_sides.1.outer = f32[2,176,256]{2,1,0:T(8,128)S(1)} custom-call(f32[2,512,128]{2,1,0:T(8,128)S(1)} %get-tuple-element.20.tiles, f32[2,144,128]{2,1,0:T(8,128)S(1)} %collective-permute-done.2.xe, f32[2,144,128]{2,1,0:T(8,128)S(1)} %collective-permute-done.3.xo, f32[272,128]{1,0:T(8,128)S(1)} %collective-permute-done.4.ye, ...), custom_call_target="tpu_custom_call" | custom-call | flops 2600000000 | bytes 4194304 | tf_op jit(solution)/shard_map/slope_sides/pallas_call | solution.py:513
  25.4 1.1 %gradient_middle.1 = (f32[256,256]{1,0:T(8,128)S(1)}, f32[3,768,128]{2,1,0:T(8,128)S(1)}) custom-call(f32[3,1024,128]{2,1,0:T(8,128)S(1)} %get-tuple-element.17.own, f32[3,200,128]{2,1,0:T(8,128)S(1)} %collective-permute-done.xe, f32[3,200,128]{2,1,0:T(8,128)S(1)} %collective-permute-done.1.xo, f32[272,128]{1,0:T(8,128)S(1)} %collective-permute-done.4.ye, ...), custom_call_target="tpu_custom_call" | custom-call | flops 1000000000 | bytes 4194304 | tf_op jit(solution)/shard_map/gradient_middle/pallas_call | solution.py:529
  26.5 0.0 collective-permute-done.6.ye
  26.5 2.2 %collective-permute-done.7.yo = f32[232,128]{1,0:T(8,128)S(1)} collective-permute-done((f32[232,128]{1,0:T(8,128)S(1)}, f32[232,128]{1,0:T(8,128)S(1)}, u32[]{:S(2)}, u32[]{:S(2)}) %collective-permute-start.7) | collective-permute-done | bytes 118816 | tf_op jit(solution)/shard_map/ppermute | solution.py:432
  28.7 3.1 %gradient_sides.1 = f32[8,64,256]{2,1,0:T(8,128)} custom-call(f32[3,768,128]{2,1,0:T(8,128)S(1)} %get-tuple-element.25.given, f32[232,128]{1,0:T(8,128)S(1)} %collective-permute-done.6.ye, f32[232,128]{1,0:T(8,128)S(1)} %collective-permute-done.7.yo, f32[4,176,256]{2,1,0:T(8,128)S(1)} %slope_middle.1.slope, f32[2,176,256]{2,1,0:T(8,128)S(1)} %slope_sides.1.outer, ...), custom_call_target="tpu_custom_call" | custom-call | flops 2000000000 | bytes 4194304 | tf_op jit(solution)/shard_map/gradient_sides/pallas_call | solution.py:539
Async XLA Ops:
  1.2 11.8 %collective-permute-start.2 = (f32[2,144,128]{2,1,0:T(8,128)S(1)}, f32[2,144,128]{2,1,0:T(8,128)S(1)}, u32[]{:S(2)}, u32[]{:S(2)}) collective-permute-start(f32[2,144,128]{2,1,0:T(8,128)S(1)} %get-tuple-element.21), channel_id=1, source_target_pairs={{0,16},{1,17},{2,18},{3,19},{4,20},{5,21},{6,22},{7,23},{8,24},{9,... | collective-permute-start | bytes 442376 | tf_op jit(solution)/shard_map/ppermute | solution.py:432
  1.3 15.7 %copy-start = (bf16[1536,256]{1,0:T(8,128)(2,1)S(1)}, bf16[1536,256]{1,0:T(8,128)(2,1)}, u32[]{:S(2)}) copy-start(bf16[1536,256]{1,0:T(8,128)(2,1)} %constant.4.clone.high_ref) | copy-start | bytes 2359300
  1.3 15.7 %copy-start.1 = (bf16[1536,256]{1,0:T(8,128)(2,1)S(1)}, bf16[1536,256]{1,0:T(8,128)(2,1)}, u32[]{:S(2)}) copy-start(bf16[1536,256]{1,0:T(8,128)(2,1)} %constant.5.clone.low_ref) | copy-start | bytes 2359300
  1.3 11.6 %collective-permute-start.3 = (f32[2,144,128]{2,1,0:T(8,128)S(1)}, f32[2,144,128]{2,1,0:T(8,128)S(1)}, u32[]{:S(2)}, u32[]{:S(2)}) collective-permute-start(f32[2,144,128]{2,1,0:T(8,128)S(1)} %get-tuple-element.22), channel_id=1, source_target_pairs={{0,1},{1,0},{2,3},{3,2},{4,5},{5,4},{6,7},{7,6},{8,9},{9,8},{10,11... | collective-permute-start | bytes 442376 | tf_op jit(solution)/shard_map/ppermute | solution.py:432
  10.9 8.6 %collective-permute-start = (f32[3,200,128]{2,1,0:T(8,128)S(1)}, f32[3,200,128]{2,1,0:T(8,128)S(1)}, u32[]{:S(2)}, u32[]{:S(2)}) collective-permute-start(f32[3,200,128]{2,1,0:T(8,128)S(1)} %get-tuple-element.18), channel_id=1, source_target_pairs={{0,16},{1,17},{2,18},{3,19},{4,20},{5,21},{6,22},{7,23},{8,24},{9,... | collective-permute-start | bytes 921608 | tf_op jit(solution)/shard_map/ppermute | solution.py:432
  11.4 8.3 %collective-permute-start.1 = (f32[3,200,128]{2,1,0:T(8,128)S(1)}, f32[3,200,128]{2,1,0:T(8,128)S(1)}, u32[]{:S(2)}, u32[]{:S(2)}) collective-permute-start(f32[3,200,128]{2,1,0:T(8,128)S(1)} %get-tuple-element.19), channel_id=1, source_target_pairs={{0,1},{1,0},{2,3},{3,2},{4,5},{5,4},{6,7},{7,6},{8,9},{9,8},{10,11... | collective-permute-start | bytes 921608 | tf_op jit(solution)/shard_map/ppermute | solution.py:432
  13.5 10.4 %collective-permute-start.4 = (f32[272,128]{1,0:T(8,128)S(1)}, f32[272,128]{1,0:T(8,128)S(1)}, u32[]{:S(2)}, u32[]{:S(2)}) collective-permute-start(f32[272,128]{1,0:T(8,128)S(1)} %get-tuple-element.23), channel_id=1, source_target_pairs={{0,1},{1,0},{2,3},{3,2},{4,5},{5,4},{6,7},{7,6},{8,9},{9,8},{10,11... | collective-permute-start | bytes 417800 | tf_op jit(solution)/shard_map/ppermute | solution.py:432
  14.0 9.9 %collective-permute-start.5 = (f32[272,128]{1,0:T(8,128)S(1)}, f32[272,128]{1,0:T(8,128)S(1)}, u32[]{:S(2)}, u32[]{:S(2)}) collective-permute-start(f32[272,128]{1,0:T(8,128)S(1)} %get-tuple-element.24), channel_id=1, source_target_pairs={{0,16},{1,2},{2,1},{3,4},{4,3},{5,6},{6,5},{7,8},{8,7},{9,10},{10,... | collective-permute-start | bytes 417800 | tf_op jit(solution)/shard_map/ppermute | solution.py:432
  20.1 6.4 %collective-permute-start.6 = (f32[232,128]{1,0:T(8,128)S(1)}, f32[232,128]{1,0:T(8,128)S(1)}, u32[]{:S(2)}, u32[]{:S(2)}) collective-permute-start(f32[232,128]{1,0:T(8,128)S(1)} %get-tuple-element.26), channel_id=1, source_target_pairs={{0,1},{1,0},{2,3},{3,2},{4,5},{5,4},{6,7},{7,6},{8,9},{9,8},{10,11... | collective-permute-start | bytes 356360 | tf_op jit(solution)/shard_map/ppermute | solution.py:432
  21.8 6.9 %collective-permute-start.7 = (f32[232,128]{1,0:T(8,128)S(1)}, f32[232,128]{1,0:T(8,128)S(1)}, u32[]{:S(2)}, u32[]{:S(2)}) collective-permute-start(f32[232,128]{1,0:T(8,128)S(1)} %get-tuple-element.27), channel_id=1, source_target_pairs={{0,16},{1,2},{2,1},{3,4},{4,3},{5,6},{6,5},{7,8},{8,7},{9,10},{10,... | collective-permute-start | bytes 356360 | tf_op jit(solution)/shard_map/ppermute | solution.py:432

commit v2 on v1

--- a/solution.py
+++ b/solution.py
@@ -24,6 +24,7 @@
 FRAME_ROWS = GROUP_ROWS + 2 * ROW_SLACK
 SIDE = ROW_SLACK + REACH
 FIRST = ROW_SLACK - REACH
+OWN_PART = 3 * SIDE * LAYERS
 NEED = ROWS + 2 * REACH
 HALO = 2 * REACH
 GROUPS = LANES // HALO
@@ -38,7 +39,7 @@
 DENSITY_QUADS = SLOPE_ROWS // LAYERS + LAGS - 1
 GRADIENT_ROWS = ROWS // QUAD * LAYERS
 GRADIENT_QUADS = ROWS // QUAD + LAGS - 1
-CHUNK = GROUP_ROWS // 2
+CHUNK = GROUP_ROWS // 3
 F32 = jnp.float32
 BF16 = jnp.bfloat16
 
@@ -100,26 +101,32 @@
     return turn(value, -first), turn(value, PIECE - first)
 
 
-def correlate_kernel(forward, adjoint, weights, rows, cols, frame, xe, xo, fields, w_smem, r_smem, c_smem, sems, small):
-    i, j, pi, pj = place()
+def correlate_part(part, forward, adjoint, weights, rows, cols, frame, out, fields, w_smem, r_smem, c_smem, sems, small):
+    i, j, pi, pj = place()
+    chunks = 2 - part
+    base = CHUNK * (pi if part == 0 else 2 - 2 * pi)
     scalars = [
         pltpu.make_async_copy(source, target, small.at[n])
         for n, (source, target) in enumerate(((weights, w_smem), (rows, r_smem), (cols, c_smem)))
     ]
 
+    def top_of(n):
+        return pl.multiple_of(base + (lax.rem(n, 2) * CHUNK if chunks == 2 else 0), CHUNK)
+
     def copies(n):
-        at = pl.ds(pl.multiple_of(lax.rem(n, 2) * CHUNK, CHUNK), CHUNK)
         return [
-            pltpu.make_async_copy(source.at[:, :, :, lax.div(n, 2), at], fields.at[k, :, :, :, n], sems.at[k, n])
+            pltpu.make_async_copy(
+                source.at[:, :, :, lax.div(n, chunks), pl.ds(top_of(n), CHUNK)], fields.at[k, :, :, :, n], sems.at[k, n]
+            )
             for k, source in enumerate((forward, adjoint))
         ]
 
     for copy in scalars:
         copy.start()
-    for n in range(2 * LAYERS):
+    for n in range(chunks * LAYERS):
         for copy in copies(jnp.int32(n)):
             copy.start()
-    frame[...] = jnp.zeros_like(frame)
+    yield
     for copy in scalars:
         copy.wait()
     down = r_smem[i] - i * ROWS + ROW_SLACK
@@ -130,11 +137,11 @@
     row = lax.broadcasted_iota(jnp.int32, (16, LANES), 0)
     turned = lax.rem(across, LANES)
 
-    @pl.loop(0, 2 * LAYERS)
+    @pl.loop(0, chunks * LAYERS)
     def _(n):
         for copy in copies(n):
             copy.wait()
-        z, top = lax.div(n, 2), lax.rem(n, 2) * CHUNK
+        z, top = lax.div(n, chunks), top_of(n)
         for r in range(0, CHUNK, 16):
             before = jnp.zeros((16, LANES), F32)
             for k in range(3):
@@ -159,36 +166,56 @@
                 before = total
                 frame[k, pl.ds((top + r + down) * LAYERS + z, 16, stride=LAYERS), :] = value
 
-    for parity, out in ((0, xe), (1, xo)):
-        start = pl.multiple_of(jnp.where(pi == parity, ROWS + FIRST, 0) * LAYERS, 8)
-        out[...] = frame[:, pl.ds(start, SIDE * LAYERS), :]
-
-
-def density_rows_kernel(flat, xe, xo, tiles, sems):
-    i, j, pi, pj = place()
-    copies = [pltpu.make_async_copy(flat.at[:, LANES * k : LANES * (k + 1)], tiles.at[k], sems.at[k]) for k in range(2)]
+    start = pl.multiple_of(jnp.where(pi == 1 - part, ROWS + FIRST, 0) * LAYERS, 8)
+    for k in range(3):
+        out[k * SIDE * LAYERS : (k + 1) * SIDE * LAYERS, :] = frame[k, pl.ds(start, SIDE * LAYERS), :]
+    yield
+
+
+def correlate_first_kernel(forward, adjoint, weights, rows, cols, flat, frame, odd, even, tiles, arriving, *scratch):
+    i, j, pi, pj = place()
+    copies = [
+        pltpu.make_async_copy(flat.at[:, LANES * k : LANES * (k + 1)], tiles.at[k], arriving.at[k]) for k in range(2)
+    ]
+    work = correlate_part(0, forward, adjoint, weights, rows, cols, frame, odd, *scratch)
+    next(work)
     for copy in copies:
         copy.start()
+    frame[...] = jnp.zeros_like(frame)
+    next(work)
     for copy in copies:
         copy.wait()
-    for parity, out in ((0, xe), (1, xo)):
+    for parity in range(2):
         start = jnp.where(pi == parity, ROWS - HALO, 0)
         for r in range(HALO):
             for k in range(2):
-                out[k, row_at(r), :] = tiles[k, pl.ds(start + r, LAYERS, stride=ROWS), :]
-
-
-def density_row(tiles, xe, xo, e, k):
+                value = tiles[k, pl.ds(start + r, LAYERS, stride=ROWS), :]
+                if parity == 0:
+                    even[k, row_at(r), :] = value
+                else:
+                    odd[OWN_PART + (k * HALO + r) * LAYERS : OWN_PART + (k * HALO + r + 1) * LAYERS, :] = value
+
+
+def correlate_second_kernel(forward, adjoint, weights, rows, cols, given, frame, out, *scratch):
+    work = correlate_part(1, forward, adjoint, weights, rows, cols, frame, out, *scratch)
+    next(work)
+    frame[...] = given[...]
+    next(work)
+
+
+def density_row(tiles, even, odd, e, k):
     i, j, pi, pj = place()
     has_up, has_down, has_left, has_right = sides_of()
     if e >= ROWS + 2 * HALO:
         return jnp.zeros((LAYERS, LANES), F32)
     if HALO <= e < HALO + ROWS:
         return tiles[k, pl.ds(e - HALO, LAYERS, stride=ROWS), :]
-    at = (k, row_at(e % (HALO + ROWS)))
+    r = e % (HALO + ROWS)
+    near, start = even[k, row_at(r), :], OWN_PART + (k * HALO + r) * LAYERS
+    far = odd[start : start + LAYERS, :]
     if e < HALO:
-        return jnp.where(has_up, chosen(pi, xo[at], xe[at]), 0.0)
-    return jnp.where(has_down, chosen(pi, xe[at], xo[at]), 0.0)
+        return jnp.where(has_up, chosen(pi, far, near), 0.0)
+    return jnp.where(has_down, chosen(pi, near, far), 0.0)
 
 
 def side_pack(frame, out, first_row, right, blocks, nines, count):
@@ -258,6 +285,9 @@
 
 
 def banded(windows, copies, count, rows, high_ref, low_ref):
+    if count > 1:
+        parts = [banded(windows.at[w : w + 1], copies.at[w : w + 1], 1, rows, high_ref, low_ref) for w in range(count)]
+        return jnp.concatenate(parts, axis=0)
     size = rows + LAYERS * (LAGS - 2)
     for w in range(count):
         for shift in range(2):
@@ -340,8 +370,9 @@
     has_up, has_down, has_left, has_right = sides_of()
     size = SIDE * LAYERS
     for k in tiles:
-        frame[k, FIRST * LAYERS : FIRST * LAYERS + size, :] += jnp.where(has_up, chosen(pi, xo[k], xe[k]), 0.0)
-        frame[k, ROWS * LAYERS : ROWS * LAYERS + size, :] += jnp.where(has_down, chosen(pi, xe[k], xo[k]), 0.0)
+        near, far = [ref[k * size : (k + 1) * size, :] for ref in (xe, xo)]
+        frame[k, FIRST * LAYERS : FIRST * LAYERS + size, :] += jnp.where(has_up, chosen(pi, far, near), 0.0)
+        frame[k, ROWS * LAYERS : ROWS * LAYERS + size, :] += jnp.where(has_down, chosen(pi, near, far), 0.0)
 
 
 def columns_kernel(own, xe, xo, ye, yo, frame):
@@ -418,19 +449,20 @@
     return other if 0 <= other < count else None
 
 
-def exchange(pair, axis):
+def exchange(value, axis, parity):
     nx, ny = lax.axis_size("gx"), lax.axis_size("gy")
-    arrived = []
-    for parity, value in enumerate(pair):
-        moves = []
-        for i in range(nx):
-            for j in range(ny):
-                to = (partner(i, nx, parity), j) if axis == "gx" else (i, partner(j, ny, parity))
-                if None in to:
-                    to = (i, j ^ 1) if axis == "gx" else (i ^ 1, j)
-                moves.append((i * ny + j, to[0] * ny + to[1]))
-        arrived.append(lax.ppermute(value, ("gx", "gy"), moves))
-    return arrived
+    moves = []
+    for i in range(nx):
+        for j in range(ny):
+            to = (partner(i, nx, parity), j) if axis == "gx" else (i, partner(j, ny, parity))
+            if None in to:
+                to = (i, j ^ 1) if axis == "gx" else (i ^ 1, j)
+            moves.append((i * ny + j, to[0] * ny + to[1]))
+    return lax.ppermute(value, ("gx", "gy"), moves)
+
+
+def exchange_both(pair, axis):
+    return [exchange(value, axis, parity) for parity, value in enumerate(pair)]
 
 
 ANY = pl.BlockSpec(memory_space=pl.ANY)
@@ -463,36 +495,48 @@
     halo = shaped(2, HALO * LAYERS, LANES)
     tile = shaped(2, LAYERS * ROWS, LANES)
     whole_frame = shaped(3, FRAME_ROWS * LAYERS, LANES)
-    *halo_rows, tiles = call(
-        density_rows_kernel, "density_rows", [ANY], [halo, halo, tile], [pltpu.SemaphoreType.DMA((2,))], 2, 0, 1
-    )(flat)
-    halo_rows = exchange(halo_rows, "gx")
-
-    side = shaped(3, SIDE * LAYERS, LANES)
-    frame, *own_rows = call(
-        correlate_kernel,
-        "correlate",
-        [ANY] * 5,
-        [whole_frame, side, side],
-        [
-            pltpu.VMEM((2, 2, 3, 3, 2 * LAYERS, CHUNK, GROUP_COLS), BF16),
-            pltpu.SMEM((2, 3), F32),
-            pltpu.SMEM(row_edges.shape, jnp.int32),
-            pltpu.SMEM(column_edges.shape, jnp.int32),
-            pltpu.SemaphoreType.DMA((2, 2 * LAYERS)),
-            pltpu.SemaphoreType.DMA((3,)),
-        ],
-        28,
-        0,
-        24,
-    )(forward, adjoint, weights, row_edges, column_edges)
-    own_rows = exchange(own_rows, "gx")
+    def correlate(kernel, name, chunks, ins, outs, scratch, mib):
+        return call(
+            kernel,
+            name,
+            ins,
+            [whole_frame] + outs,
+            scratch
+            + [
+                pltpu.VMEM((2, 2, 3, 3, chunks * LAYERS, CHUNK, GROUP_COLS), BF16),
+                pltpu.SMEM((2, 3), F32),
+                pltpu.SMEM(row_edges.shape, jnp.int32),
+                pltpu.SMEM(column_edges.shape, jnp.int32),
+                pltpu.SemaphoreType.DMA((2, chunks * LAYERS)),
+                pltpu.SemaphoreType.DMA((3,)),
+            ],
+            mib,
+            0,
+            8 * chunks,
+        )
+
+    given = (forward, adjoint, weights, row_edges, column_edges)
+    frame, odd, even, tiles = correlate(
+        correlate_first_kernel,
+        "correlate_first",
+        2,
+        [ANY] * 6,
+        [shaped(OWN_PART + 2 * HALO * LAYERS, LANES), halo, tile],
+        [pltpu.SemaphoreType.DMA((2,))],
+        20,
+    )(*given, flat)
+    odd = exchange(odd, "gx", 1)
+    halo_rows = [exchange(even, "gx", 0), odd]
+    frame, own_even = correlate(
+        correlate_second_kernel, "correlate_second", 1, [ANY] * 5 + [VMEM], [shaped(OWN_PART, LANES)], [], 14
+    )(*given, frame)
+    own_rows = [exchange(own_even, "gx", 0), odd]
 
     column = shaped(DENSITY_PART + side_size(INNER_SIDE), LANES)
     columns = call(first_columns_kernel, "first_columns", [VMEM] * 4, [column, column], [], 2, 0, 30)(
         tiles, *halo_rows, frame
     )
-    columns = exchange(columns, "gy")
+    columns = exchange_both(columns, "gy")
 
     def work(count, quads, rows):
         return [
@@ -524,7 +568,7 @@
     own_frame = pltpu.VMEM((3, GROUP_ROWS * LAYERS, LANES), F32)
     packed = shaped(side_size(OUTER_SIDE), LANES)
     own_columns = call(columns_kernel, "columns", [VMEM] * 3, [packed, packed], [own_frame], 4, 0, 4)(frame, *own_rows)
-    own_columns = exchange(own_columns, "gy")
+    own_columns = exchange_both(own_columns, "gy")
 
     middle, frame = call(
         gradient_middle_kernel,

time: 31.9 us -> 30.2 us (0.947)
  starting transfers between devices: 11.2 us -> 8.21 us
  Pallas kernels: 18 us -> 18.6 us
  waiting for transfers between devices: 2.52 us -> 3.08 us
    ppermute x8 -> x7, starting transfers between devices: 11.2 us -> 8.21 us  [exchange(): return lax.ppermute(value, ('gx', 'gy'), moves)]
    pallas_call x2, Pallas kernels: 9.07 us -> 9.78 us  [the longest x1 6.09 us: body(): correlate(correlate_first_kernel, 'correlate_first', 2, [ANY] * 6, [shape...]
    ppermute x8 -> x7, waiting for transfers between devices: 2.52 us -> 3.08 us  [exchange(): return lax.ppermute(value, ('gx', 'gy'), moves)]
  transfers between devices with their start and end apart: 8 -> 7, of which waited for: 2 -> 3; matrix products, arithmetic and copies ran while one was open for 0% -> 0% of each run, Pallas kernels for 43% -> 32%
where the time goes in v2:
time: 30.2 us; the launch traced here: 30 us
  Pallas kernels  18.6 us (62%)
  starting transfers between devices  8.21 us (27%)
  waiting for transfers between devices  3.08 us (10%)
    ppermute x7, starting transfers between devices, exchange(): return lax.ppermute(value, ('gx', 'gy'), moves)  8.21 us
    pallas_call x1, Pallas kernels, body(): correlate(correlate_first_kernel, 'correlate_first', 2, [ANY] * 6, [shape...  6.09 us
    pallas_call x1, Pallas kernels, body(): correlate(correlate_second_kernel, 'correlate_second', 1, [ANY] * 5 + [VM...  3.68 us
    ppermute x7, waiting for transfers between devices, exchange(): return lax.ppermute(value, ('gx', 'gy'), moves)  3.08 us
    pallas_call x1, Pallas kernels, body(): call(gradient_sides_kernel, 'gradient_sides', [VMEM] * 8, shaped(*density...  2.92 us
    pallas_call x1, Pallas kernels, body(): call(slope_middle_kernel, 'slope_middle', [VMEM] * 5, shaped(len(MIDDLE_S...  2.39 us
    pallas_call x1, Pallas kernels, body(): call(slope_sides_kernel, 'slope_sides', [VMEM] * 7, shaped(2, SLOPE_ROWS,...  1.56 us
    pallas_call x1, Pallas kernels, body(): call(gradient_middle_kernel, 'gradient_middle', [VMEM] * 8, [shaped(len(M...  1.09 us
  transfers between devices with their start and end apart: 7, of which 3 were waited for; matrix products, arithmetic and copies ran while one was open for 0% of the time, Pallas kernels for 32%

profile of v2, /device:TPU:2, one launch (start us, length us, event | category | flops | bytes accessed | tf_op | source)
XLA Modules:
  0.0 30.0 jit_solution(8172886818717505068)
XLA Ops:
  0.0 6.1 %correlate_first.1 = (f32[3,1024,128]{2,1,0:T(8,128)S(1)}, f32[888,128]{1,0:T(8,128)S(1)}, f32[2,144,128]{2,1,0:T(8,128)S(1)}, f32[2,512,128]{2,1,0:T(8,128)S(1)}) custom-call(bf16[2,3,3,8,96,384]{5,4,3,2,1,0:T(8,128)(2,1)} %forward.3, bf16[2,3,3,8,96,384]{5,4,3,2,1,0:T(8,128)(2,1)} %adjoint.3, f32[2,3]{1,0:T(2,128)} %weights.3, s32[9]{0:T(128)} %rows.3, ...), custom_call_target="tpu_custom_call" | custom-call | bytes 16777216 | tf_op jit(solution)/shard_map/correlate_first/pallas_call | solution.py:519
  6.1 1.7 %collective-permute-start.1 = (f32[888,128]{1,0:T(8,128)S(1)}, f32[888,128]{1,0:T(8,128)S(1)}, u32[]{:S(2)}, u32[]{:S(2)}) collective-permute-start(f32[888,128]{1,0:T(8,128)S(1)} %get-tuple-element.20), channel_id=1, source_target_pairs={{0,1},{1,0},{2,3},{3,2},{4,5},{5,4},{6,7},{7,6},{8,9},{9,8},{10,11... | collective-permute-start | bytes 1363976 | tf_op jit(solution)/shard_map/ppermute | solution.py:461
  7.8 3.7 %correlate_second.1 = (f32[3,1024,128]{2,1,0:T(8,128)S(1)}, f32[600,128]{1,0:T(8,128)S(1)}) custom-call(bf16[2,3,3,8,96,384]{5,4,3,2,1,0:T(8,128)(2,1)} %forward.3, bf16[2,3,3,8,96,384]{5,4,3,2,1,0:T(8,128)(2,1)} %adjoint.3, f32[2,3]{1,0:T(2,128)} %weights.3, s32[9]{0:T(128)} %rows.3, s32[17]{0:T(128)} %cols.3, f32[3,1024,128]{2,1,0:T(8,128)S(1)} %get-tuple-element.17.given), custom_call_target="tpu_custom_call" | custom-call | bytes 8388608 | tf_op jit(solution)/shard_map/correlate_second/pallas_call | solution.py:530
  11.4 0.4 %collective-permute-start = (f32[600,128]{1,0:T(8,128)S(1)}, f32[600,128]{1,0:T(8,128)S(1)}, u32[]{:S(2)}, u32[]{:S(2)}) collective-permute-start(f32[600,128]{1,0:T(8,128)S(1)} %get-tuple-element.19), channel_id=1, source_target_pairs={{0,16},{1,17},{2,18},{3,19},{4,20},{5,21},{6,22},{7,23},{8,24},{9,... | collective-permute-start | bytes 921608 | tf_op jit(solution)/shard_map/ppermute | solution.py:461
  11.8 0.2 collective-permute-start.2
  12.0 1.3 %collective-permute-done.2.xe = f32[2,144,128]{2,1,0:T(8,128)S(1)} collective-permute-done((f32[2,144,128]{2,1,0:T(8,128)S(1)}, f32[2,144,128]{2,1,0:T(8,128)S(1)}, u32[]{:S(2)}, u32[]{:S(2)}) %collective-permute-start.2) | collective-permute-done | bytes 147488 | tf_op jit(solution)/shard_map/ppermute | solution.py:461
  13.3 1.3 %collective-permute-done.1.xo = f32[888,128]{1,0:T(8,128)S(1)} collective-permute-done((f32[888,128]{1,0:T(8,128)S(1)}, f32[888,128]{1,0:T(8,128)S(1)}, u32[]{:S(2)}, u32[]{:S(2)}) %collective-permute-start.1) | collective-permute-done | bytes 454688 | tf_op jit(solution)/shard_map/ppermute | solution.py:461
  14.6 0.5 %first_columns.1 = (f32[272,128]{1,0:T(8,128)S(1)}, f32[272,128]{1,0:T(8,128)S(1)}) custom-call(f32[2,512,128]{2,1,0:T(8,128)S(1)} %get-tuple-element.21.tiles, f32[2,144,128]{2,1,0:T(8,128)S(1)} %collective-permute-done.2.xe, f32[888,128]{1,0:T(8,128)S(1)} %collective-permute-done.1.xo, f32[3,1024,128]{2,1,0:T(8,128)S(1)} %get-tuple-element.18.own), custom_call_target="tpu_custom_call" | custom-call | bytes 31457280 | tf_op jit(solution)/shard_map/first_columns/pallas_call | solution.py:536
  15.2 0.0 copy-start
  15.2 0.0 copy-start.1
  15.2 1.7 %collective-permute-start.3 = (f32[272,128]{1,0:T(8,128)S(1)}, f32[272,128]{1,0:T(8,128)S(1)}, u32[]{:S(2)}, u32[]{:S(2)}) collective-permute-start(f32[272,128]{1,0:T(8,128)S(1)} %get-tuple-element.23), channel_id=1, source_target_pairs={{0,1},{1,0},{2,3},{3,2},{4,5},{5,4},{6,7},{7,6},{8,9},{9,8},{10,11... | collective-permute-start | bytes 417800 | tf_op jit(solution)/shard_map/ppermute | solution.py:461
  16.8 2.2 %collective-permute-start.4 = (f32[272,128]{1,0:T(8,128)S(1)}, f32[272,128]{1,0:T(8,128)S(1)}, u32[]{:S(2)}, u32[]{:S(2)}) collective-permute-start(f32[272,128]{1,0:T(8,128)S(1)} %get-tuple-element.24), channel_id=1, source_target_pairs={{0,16},{1,2},{2,1},{3,4},{4,3},{5,6},{6,5},{7,8},{8,7},{9,10},{10,... | collective-permute-start | bytes 417800 | tf_op jit(solution)/shard_map/ppermute | solution.py:461
  19.0 0.0 collective-permute-done.xe
  19.0 0.4 %columns.1 = (f32[232,128]{1,0:T(8,128)S(1)}, f32[232,128]{1,0:T(8,128)S(1)}) custom-call(f32[3,1024,128]{2,1,0:T(8,128)S(1)} %get-tuple-element.18.own, f32[600,128]{1,0:T(8,128)S(1)} %collective-permute-done.xe, f32[888,128]{1,0:T(8,128)S(1)} %collective-permute-done.1.xo), custom_call_target="tpu_custom_call" | custom-call | bytes 4194304 | tf_op jit(solution)/shard_map/columns/pallas_call | solution.py:570
  19.4 0.8 %collective-permute-start.5 = (f32[232,128]{1,0:T(8,128)S(1)}, f32[232,128]{1,0:T(8,128)S(1)}, u32[]{:S(2)}, u32[]{:S(2)}) collective-permute-start(f32[232,128]{1,0:T(8,128)S(1)} %get-tuple-element.26), channel_id=1, source_target_pairs={{0,1},{1,0},{2,3},{3,2},{4,5},{5,4},{6,7},{7,6},{8,9},{9,8},{10,11... | collective-permute-start | bytes 356360 | tf_op jit(solution)/shard_map/ppermute | solution.py:461
  20.1 1.4 %collective-permute-start.6 = (f32[232,128]{1,0:T(8,128)S(1)}, f32[232,128]{1,0:T(8,128)S(1)}, u32[]{:S(2)}, u32[]{:S(2)}) collective-permute-start(f32[232,128]{1,0:T(8,128)S(1)} %get-tuple-element.27), channel_id=1, source_target_pairs={{0,16},{1,2},{2,1},{3,4},{4,3},{5,6},{6,5},{7,8},{8,7},{9,10},{10,... | collective-permute-start | bytes 356360 | tf_op jit(solution)/shard_map/ppermute | solution.py:461
  21.5 0.0 copy-done
  21.5 0.0 copy-done.1
  21.5 2.4 %slope_middle.1.slope = f32[4,176,256]{2,1,0:T(8,128)S(1)} custom-call(f32[2,512,128]{2,1,0:T(8,128)S(1)} %get-tuple-element.21.tiles, f32[2,144,128]{2,1,0:T(8,128)S(1)} %collective-permute-done.2.xe, f32[888,128]{1,0:T(8,128)S(1)} %collective-permute-done.1.xo, bf16[1536,256]{1,0:T(8,128)(2,1)S(1)} %copy-done, bf16[1536,256]{1,0:T(8,128)(2,1)S(1)} %copy-done.1), custom_call_target="tpu_custom_call" | custom-call | flops 99999997952 | bytes 314572800 | tf_op jit(solution)/shard_map/slope_middle/pallas_call | solution.py:547
  23.9 0.0 collective-permute-done.3.ye
  23.9 0.5 %collective-permute-done.4.yo = f32[272,128]{1,0:T(8,128)S(1)} collective-permute-done((f32[272,128]{1,0:T(8,128)S(1)}, f32[272,128]{1,0:T(8,128)S(1)}, u32[]{:S(2)}, u32[]{:S(2)}) %collective-permute-start.4) | collective-permute-done | bytes 139296 | tf_op jit(solution)/shard_map/ppermute | solution.py:461
  24.4 1.6 %slope_sides.1.outer = f32[2,176,256]{2,1,0:T(8,128)S(1)} custom-call(f32[2,512,128]{2,1,0:T(8,128)S(1)} %get-tuple-element.21.tiles, f32[2,144,128]{2,1,0:T(8,128)S(1)} %collective-permute-done.2.xe, f32[888,128]{1,0:T(8,128)S(1)} %collective-permute-done.1.xo, f32[272,128]{1,0:T(8,128)S(1)} %collective-permute-done.3.ye, ...), custom_call_target="tpu_custom_call" | custom-call | flops 2600000000 | bytes 4194304 | tf_op jit(solution)/shard_map/slope_sides/pallas_call | solution.py:557
  26.0 1.1 %gradient_middle.1 = (f32[256,256]{1,0:T(8,128)S(1)}, f32[3,768,128]{2,1,0:T(8,128)S(1)}) custom-call(f32[3,1024,128]{2,1,0:T(8,128)S(1)} %get-tuple-element.18.own, f32[600,128]{1,0:T(8,128)S(1)} %collective-permute-done.xe, f32[888,128]{1,0:T(8,128)S(1)} %collective-permute-done.1.xo, f32[272,128]{1,0:T(8,128)S(1)} %collective-permute-done.3.ye, ...), custom_call_target="tpu_custom_call" | custom-call | flops 1000000000 | bytes 4194304 | tf_op jit(solution)/shard_map/gradient_middle/pallas_call | solution.py:573
  27.1 0.0 collective-permute-done.5.ye
  27.1 0.0 collective-permute-done.6.yo
  27.1 2.9 %gradient_sides.1 = f32[8,64,256]{2,1,0:T(8,128)} custom-call(f32[3,768,128]{2,1,0:T(8,128)S(1)} %get-tuple-element.25.given, f32[232,128]{1,0:T(8,128)S(1)} %collective-permute-done.5.ye, f32[232,128]{1,0:T(8,128)S(1)} %collective-permute-done.6.yo, f32[4,176,256]{2,1,0:T(8,128)S(1)} %slope_middle.1.slope, f32[2,176,256]{2,1,0:T(8,128)S(1)} %slope_sides.1.outer, ...), custom_call_target="tpu_custom_call" | custom-call | flops 2000000000 | bytes 4194304 | tf_op jit(solution)/shard_map/gradient_sides/pallas_call | solution.py:583
Async XLA Ops:
  6.1 8.5 %collective-permute-start.1 = (f32[888,128]{1,0:T(8,128)S(1)}, f32[888,128]{1,0:T(8,128)S(1)}, u32[]{:S(2)}, u32[]{:S(2)}) collective-permute-start(f32[888,128]{1,0:T(8,128)S(1)} %get-tuple-element.20), channel_id=1, source_target_pairs={{0,1},{1,0},{2,3},{3,2},{4,5},{5,4},{6,7},{7,6},{8,9},{9,8},{10,11... | collective-permute-start | bytes 1363976 | tf_op jit(solution)/shard_map/ppermute | solution.py:461
  11.4 7.5 %collective-permute-start = (f32[600,128]{1,0:T(8,128)S(1)}, f32[600,128]{1,0:T(8,128)S(1)}, u32[]{:S(2)}, u32[]{:S(2)}) collective-permute-start(f32[600,128]{1,0:T(8,128)S(1)} %get-tuple-element.19), channel_id=1, source_target_pairs={{0,16},{1,17},{2,18},{3,19},{4,20},{5,21},{6,22},{7,23},{8,24},{9,... | collective-permute-start | bytes 921608 | tf_op jit(solution)/shard_map/ppermute | solution.py:461
  11.8 1.5 %collective-permute-start.2 = (f32[2,144,128]{2,1,0:T(8,128)S(1)}, f32[2,144,128]{2,1,0:T(8,128)S(1)}, u32[]{:S(2)}, u32[]{:S(2)}) collective-permute-start(f32[2,144,128]{2,1,0:T(8,128)S(1)} %get-tuple-element.22), channel_id=1, source_target_pairs={{0,16},{1,17},{2,18},{3,19},{4,20},{5,21},{6,22},{7,23},{8,24},{9,... | collective-permute-start | bytes 442376 | tf_op jit(solution)/shard_map/ppermute | solution.py:461
  15.2 6.4 %copy-start = (bf16[1536,256]{1,0:T(8,128)(2,1)S(1)}, bf16[1536,256]{1,0:T(8,128)(2,1)}, u32[]{:S(2)}) copy-start(bf16[1536,256]{1,0:T(8,128)(2,1)} %constant.4.clone.high_ref) | copy-start | bytes 2359300
  15.2 6.4 %copy-start.1 = (bf16[1536,256]{1,0:T(8,128)(2,1)S(1)}, bf16[1536,256]{1,0:T(8,128)(2,1)}, u32[]{:S(2)}) copy-start(bf16[1536,256]{1,0:T(8,128)(2,1)} %constant.5.clone.low_ref) | copy-start | bytes 2359300
  15.2 8.7 %collective-permute-start.3 = (f32[272,128]{1,0:T(8,128)S(1)}, f32[272,128]{1,0:T(8,128)S(1)}, u32[]{:S(2)}, u32[]{:S(2)}) collective-permute-start(f32[272,128]{1,0:T(8,128)S(1)} %get-tuple-element.23), channel_id=1, source_target_pairs={{0,1},{1,0},{2,3},{3,2},{4,5},{5,4},{6,7},{7,6},{8,9},{9,8},{10,11... | collective-permute-start | bytes 417800 | tf_op jit(solution)/shard_map/ppermute | solution.py:461
  16.8 7.6 %collective-permute-start.4 = (f32[272,128]{1,0:T(8,128)S(1)}, f32[272,128]{1,0:T(8,128)S(1)}, u32[]{:S(2)}, u32[]{:S(2)}) collective-permute-start(f32[272,128]{1,0:T(8,128)S(1)} %get-tuple-element.24), channel_id=1, source_target_pairs={{0,16},{1,2},{2,1},{3,4},{4,3},{5,6},{6,5},{7,8},{8,7},{9,10},{10,... | collective-permute-start | bytes 417800 | tf_op jit(solution)/shard_map/ppermute | solution.py:461
  19.4 7.7 %collective-permute-start.5 = (f32[232,128]{1,0:T(8,128)S(1)}, f32[232,128]{1,0:T(8,128)S(1)}, u32[]{:S(2)}, u32[]{:S(2)}) collective-permute-start(f32[232,128]{1,0:T(8,128)S(1)} %get-tuple-element.26), channel_id=1, source_target_pairs={{0,1},{1,0},{2,3},{3,2},{4,5},{5,4},{6,7},{7,6},{8,9},{9,8},{10,11... | collective-permute-start | bytes 356360 | tf_op jit(solution)/shard_map/ppermute | solution.py:461
  20.1 6.9 %collective-permute-start.6 = (f32[232,128]{1,0:T(8,128)S(1)}, f32[232,128]{1,0:T(8,128)S(1)}, u32[]{:S(2)}, u32[]{:S(2)}) collective-permute-start(f32[232,128]{1,0:T(8,128)S(1)} %get-tuple-element.27), channel_id=1, source_target_pairs={{0,16},{1,2},{2,1},{3,4},{4,3},{5,6},{6,5},{7,8},{8,7},{9,10},{10,... | collective-permute-start | bytes 356360 | tf_op jit(solution)/shard_map/ppermute | solution.py:461

commit v3 on v2

--- a/solution.py
+++ b/solution.py
@@ -395,13 +395,13 @@
     side_unpack(frame, pick(ye, yo), first_row, 2, has_right, *side)
 
 
-def weigh(frame, windows, n, w, slope, before):
+def weigh(tiles, windows, n, w, slope, before):
     lane = lane_of(LAYERS)
     lower = lane < PIECE
     own = jnp.where(lower, lane, lane - PIECE) >= 2 * REACH
     for e in range(0, QUAD * GRADIENT_QUADS, 2):
         at = half_at(e)
-        even, odd = [[frame[k, row_at(FIRST + e + h), :] for k in range(3)] for h in range(2)]
+        even, odd = [[tile[row_at(FIRST + e + h), :] for tile in tiles] for h in range(2)]
         start = STARTS[w] - REACH + COL_SLACK
         factor = slope[at] if before is None else jnp.where(own, slope[at], turn(before[at], -SPAN))
         windows[(n,) + at] = jnp.where(lower, piece_of(even, start)[0], piece_of(odd, start)[1]) * factor
@@ -411,18 +411,20 @@
     frame[...] = own[:, 0 : GROUP_ROWS * LAYERS, :]
     add_rows(frame, xe, xo, range(3))
     for n, w in enumerate(MIDDLE):
-        weigh(frame, windows, n, w, slope.at[w - 1], slope.at[w - 2])
+        weigh([frame.at[k] for k in range(3)], windows, n, w, slope.at[w - 1], slope.at[w - 2])
     out[...] = banded(windows, copies, len(MIDDLE), GRADIENT_ROWS, high_ref, low_ref)
     add_columns(frame, ye, yo, DENSITY_PART, INNER_SIDE)
 
 
 def gradient_sides_kernel(given, ye, yo, slope, outer, middle, high_ref, low_ref, out, frame, windows, copies, result):
-    frame[...] = given[...]
+    for k in (0, 2):
+        frame[k] = given[k]
     add_columns(frame, ye, yo, 0, OUTER_SIDE)
-    weigh(frame, windows, 0, 0, outer.at[0], None)
-    weigh(frame, windows, 1, 1, slope.at[0], outer.at[0])
-    weigh(frame, windows, 2, 4, slope.at[3], slope.at[2])
-    weigh(frame, windows, 3, 5, outer.at[1], slope.at[3])
+    frame_tiles = (frame.at[0], given.at[1], frame.at[2])
+    weigh(frame_tiles, windows, 0, 0, outer.at[0], None)
+    weigh(frame_tiles, windows, 1, 1, slope.at[0], outer.at[0])
+    weigh(frame_tiles, windows, 2, 4, slope.at[3], slope.at[2])
+    weigh(frame_tiles, windows, 3, 5, outer.at[1], slope.at[3])
     result[...] = banded(windows, copies, 4, GRADIENT_ROWS, high_ref, low_ref)
     lane = lane_of(LAYERS)
     places = ((result, 0), (result, 1), (middle, 0), (middle, 1), (result, 2), (result, 3))

time: 30.2 us -> 30.2 us (level)
  no operation moved by 1% of the time
where the time goes in v3:
time: 30.2 us; the launch traced here: 30 us
  Pallas kernels  18.6 us (62%)
  starting transfers between devices  8.21 us (27%)
  waiting for transfers between devices  3.08 us (10%)
    ppermute x7, starting transfers between devices, exchange(): return lax.ppermute(value, ('gx', 'gy'), moves)  8.21 us
    pallas_call x1, Pallas kernels, body(): correlate(correlate_first_kernel, 'correlate_first', 2, [ANY] * 6, [shape...  6.09 us
    pallas_call x1, Pallas kernels, body(): correlate(correlate_second_kernel, 'correlate_second', 1, [ANY] * 5 + [VM...  3.68 us
    ppermute x7, waiting for transfers between devices, exchange(): return lax.ppermute(value, ('gx', 'gy'), moves)  3.08 us
    pallas_call x1, Pallas kernels, body(): call(gradient_sides_kernel, 'gradient_sides', [VMEM] * 8, shaped(*density...  2.91 us
    pallas_call x1, Pallas kernels, body(): call(slope_middle_kernel, 'slope_middle', [VMEM] * 5, shaped(len(MIDDLE_S...  2.39 us
    pallas_call x1, Pallas kernels, body(): call(slope_sides_kernel, 'slope_sides', [VMEM] * 7, shaped(2, SLOPE_ROWS,...  1.56 us
    pallas_call x1, Pallas kernels, body(): call(gradient_middle_kernel, 'gradient_middle', [VMEM] * 8, [shaped(len(M...  1.09 us
  transfers between devices with their start and end apart: 7, of which 3 were waited for; matrix products, arithmetic and copies ran while one was open for 0% of the time, Pallas kernels for 32%

profile of v3, /device:TPU:2, one launch (start us, length us, event | category | flops | bytes accessed | tf_op | source)
XLA Modules:
  0.0 30.0 jit_solution(14299826508990078080)
XLA Ops:
  0.0 6.1 %correlate_first.1 = (f32[3,1024,128]{2,1,0:T(8,128)S(1)}, f32[888,128]{1,0:T(8,128)S(1)}, f32[2,144,128]{2,1,0:T(8,128)S(1)}, f32[2,512,128]{2,1,0:T(8,128)S(1)}) custom-call(bf16[2,3,3,8,96,384]{5,4,3,2,1,0:T(8,128)(2,1)} %forward.3, bf16[2,3,3,8,96,384]{5,4,3,2,1,0:T(8,128)(2,1)} %adjoint.3, f32[2,3]{1,0:T(2,128)} %weights.3, s32[9]{0:T(128)} %rows.3, ...), custom_call_target="tpu_custom_call" | custom-call | bytes 16777216 | tf_op jit(solution)/shard_map/correlate_first/pallas_call | solution.py:521
  6.1 1.7 %collective-permute-start.1 = (f32[888,128]{1,0:T(8,128)S(1)}, f32[888,128]{1,0:T(8,128)S(1)}, u32[]{:S(2)}, u32[]{:S(2)}) collective-permute-start(f32[888,128]{1,0:T(8,128)S(1)} %get-tuple-element.20), channel_id=1, source_target_pairs={{0,1},{1,0},{2,3},{3,2},{4,5},{5,4},{6,7},{7,6},{8,9},{9,8},{10,11... | collective-permute-start | bytes 1363976 | tf_op jit(solution)/shard_map/ppermute | solution.py:463
  7.8 3.7 %correlate_second.1 = (f32[3,1024,128]{2,1,0:T(8,128)S(1)}, f32[600,128]{1,0:T(8,128)S(1)}) custom-call(bf16[2,3,3,8,96,384]{5,4,3,2,1,0:T(8,128)(2,1)} %forward.3, bf16[2,3,3,8,96,384]{5,4,3,2,1,0:T(8,128)(2,1)} %adjoint.3, f32[2,3]{1,0:T(2,128)} %weights.3, s32[9]{0:T(128)} %rows.3, s32[17]{0:T(128)} %cols.3, f32[3,1024,128]{2,1,0:T(8,128)S(1)} %get-tuple-element.17.given), custom_call_target="tpu_custom_call" | custom-call | bytes 8388608 | tf_op jit(solution)/shard_map/correlate_second/pallas_call | solution.py:532
  11.4 0.4 %collective-permute-start = (f32[600,128]{1,0:T(8,128)S(1)}, f32[600,128]{1,0:T(8,128)S(1)}, u32[]{:S(2)}, u32[]{:S(2)}) collective-permute-start(f32[600,128]{1,0:T(8,128)S(1)} %get-tuple-element.19), channel_id=1, source_target_pairs={{0,16},{1,17},{2,18},{3,19},{4,20},{5,21},{6,22},{7,23},{8,24},{9,... | collective-permute-start | bytes 921608 | tf_op jit(solution)/shard_map/ppermute | solution.py:463
  11.8 0.2 collective-permute-start.2
  12.0 1.3 %collective-permute-done.2.xe = f32[2,144,128]{2,1,0:T(8,128)S(1)} collective-permute-done((f32[2,144,128]{2,1,0:T(8,128)S(1)}, f32[2,144,128]{2,1,0:T(8,128)S(1)}, u32[]{:S(2)}, u32[]{:S(2)}) %collective-permute-start.2) | collective-permute-done | bytes 147488 | tf_op jit(solution)/shard_map/ppermute | solution.py:463
  13.3 1.3 %collective-permute-done.1.xo = f32[888,128]{1,0:T(8,128)S(1)} collective-permute-done((f32[888,128]{1,0:T(8,128)S(1)}, f32[888,128]{1,0:T(8,128)S(1)}, u32[]{:S(2)}, u32[]{:S(2)}) %collective-permute-start.1) | collective-permute-done | bytes 454688 | tf_op jit(solution)/shard_map/ppermute | solution.py:463
  14.6 0.5 %first_columns.1 = (f32[272,128]{1,0:T(8,128)S(1)}, f32[272,128]{1,0:T(8,128)S(1)}) custom-call(f32[2,512,128]{2,1,0:T(8,128)S(1)} %get-tuple-element.21.tiles, f32[2,144,128]{2,1,0:T(8,128)S(1)} %collective-permute-done.2.xe, f32[888,128]{1,0:T(8,128)S(1)} %collective-permute-done.1.xo, f32[3,1024,128]{2,1,0:T(8,128)S(1)} %get-tuple-element.18.own), custom_call_target="tpu_custom_call" | custom-call | bytes 31457280 | tf_op jit(solution)/shard_map/first_columns/pallas_call | solution.py:538
  15.2 0.0 copy-start
  15.2 0.0 copy-start.1
  15.2 1.7 %collective-permute-start.3 = (f32[272,128]{1,0:T(8,128)S(1)}, f32[272,128]{1,0:T(8,128)S(1)}, u32[]{:S(2)}, u32[]{:S(2)}) collective-permute-start(f32[272,128]{1,0:T(8,128)S(1)} %get-tuple-element.23), channel_id=1, source_target_pairs={{0,1},{1,0},{2,3},{3,2},{4,5},{5,4},{6,7},{7,6},{8,9},{9,8},{10,11... | collective-permute-start | bytes 417800 | tf_op jit(solution)/shard_map/ppermute | solution.py:463
  16.8 2.2 %collective-permute-start.4 = (f32[272,128]{1,0:T(8,128)S(1)}, f32[272,128]{1,0:T(8,128)S(1)}, u32[]{:S(2)}, u32[]{:S(2)}) collective-permute-start(f32[272,128]{1,0:T(8,128)S(1)} %get-tuple-element.24), channel_id=1, source_target_pairs={{0,16},{1,2},{2,1},{3,4},{4,3},{5,6},{6,5},{7,8},{8,7},{9,10},{10,... | collective-permute-start | bytes 417800 | tf_op jit(solution)/shard_map/ppermute | solution.py:463
  19.0 0.0 collective-permute-done.xe
  19.0 0.4 %columns.1 = (f32[232,128]{1,0:T(8,128)S(1)}, f32[232,128]{1,0:T(8,128)S(1)}) custom-call(f32[3,1024,128]{2,1,0:T(8,128)S(1)} %get-tuple-element.18.own, f32[600,128]{1,0:T(8,128)S(1)} %collective-permute-done.xe, f32[888,128]{1,0:T(8,128)S(1)} %collective-permute-done.1.xo), custom_call_target="tpu_custom_call" | custom-call | bytes 4194304 | tf_op jit(solution)/shard_map/columns/pallas_call | solution.py:572
  19.4 0.8 %collective-permute-start.5 = (f32[232,128]{1,0:T(8,128)S(1)}, f32[232,128]{1,0:T(8,128)S(1)}, u32[]{:S(2)}, u32[]{:S(2)}) collective-permute-start(f32[232,128]{1,0:T(8,128)S(1)} %get-tuple-element.26), channel_id=1, source_target_pairs={{0,1},{1,0},{2,3},{3,2},{4,5},{5,4},{6,7},{7,6},{8,9},{9,8},{10,11... | collective-permute-start | bytes 356360 | tf_op jit(solution)/shard_map/ppermute | solution.py:463
  20.1 1.4 %collective-permute-start.6 = (f32[232,128]{1,0:T(8,128)S(1)}, f32[232,128]{1,0:T(8,128)S(1)}, u32[]{:S(2)}, u32[]{:S(2)}) collective-permute-start(f32[232,128]{1,0:T(8,128)S(1)} %get-tuple-element.27), channel_id=1, source_target_pairs={{0,16},{1,2},{2,1},{3,4},{4,3},{5,6},{6,5},{7,8},{8,7},{9,10},{10,... | collective-permute-start | bytes 356360 | tf_op jit(solution)/shard_map/ppermute | solution.py:463
  21.5 0.0 copy-done
  21.5 0.0 copy-done.1
  21.5 2.4 %slope_middle.1.slope = f32[4,176,256]{2,1,0:T(8,128)S(1)} custom-call(f32[2,512,128]{2,1,0:T(8,128)S(1)} %get-tuple-element.21.tiles, f32[2,144,128]{2,1,0:T(8,128)S(1)} %collective-permute-done.2.xe, f32[888,128]{1,0:T(8,128)S(1)} %collective-permute-done.1.xo, bf16[1536,256]{1,0:T(8,128)(2,1)S(1)} %copy-done, bf16[1536,256]{1,0:T(8,128)(2,1)S(1)} %copy-done.1), custom_call_target="tpu_custom_call" | custom-call | flops 99999997952 | bytes 314572800 | tf_op jit(solution)/shard_map/slope_middle/pallas_call | solution.py:549
  23.9 0.0 collective-permute-done.3.ye
  23.9 0.5 %collective-permute-done.4.yo = f32[272,128]{1,0:T(8,128)S(1)} collective-permute-done((f32[272,128]{1,0:T(8,128)S(1)}, f32[272,128]{1,0:T(8,128)S(1)}, u32[]{:S(2)}, u32[]{:S(2)}) %collective-permute-start.4) | collective-permute-done | bytes 139296 | tf_op jit(solution)/shard_map/ppermute | solution.py:463
  24.4 1.6 %slope_sides.1.outer = f32[2,176,256]{2,1,0:T(8,128)S(1)} custom-call(f32[2,512,128]{2,1,0:T(8,128)S(1)} %get-tuple-element.21.tiles, f32[2,144,128]{2,1,0:T(8,128)S(1)} %collective-permute-done.2.xe, f32[888,128]{1,0:T(8,128)S(1)} %collective-permute-done.1.xo, f32[272,128]{1,0:T(8,128)S(1)} %collective-permute-done.3.ye, ...), custom_call_target="tpu_custom_call" | custom-call | flops 2600000000 | bytes 4194304 | tf_op jit(solution)/shard_map/slope_sides/pallas_call | solution.py:559
  26.0 1.1 %gradient_middle.1 = (f32[256,256]{1,0:T(8,128)S(1)}, f32[3,768,128]{2,1,0:T(8,128)S(1)}) custom-call(f32[3,1024,128]{2,1,0:T(8,128)S(1)} %get-tuple-element.18.own, f32[600,128]{1,0:T(8,128)S(1)} %collective-permute-done.xe, f32[888,128]{1,0:T(8,128)S(1)} %collective-permute-done.1.xo, f32[272,128]{1,0:T(8,128)S(1)} %collective-permute-done.3.ye, ...), custom_call_target="tpu_custom_call" | custom-call | flops 1000000000 | bytes 4194304 | tf_op jit(solution)/shard_map/gradient_middle/pallas_call | solution.py:575
  27.1 0.0 collective-permute-done.5.ye
  27.1 0.0 collective-permute-done.6.yo
  27.1 2.9 %gradient_sides.1 = f32[8,64,256]{2,1,0:T(8,128)} custom-call(f32[3,768,128]{2,1,0:T(8,128)S(1)} %get-tuple-element.25.given, f32[232,128]{1,0:T(8,128)S(1)} %collective-permute-done.5.ye, f32[232,128]{1,0:T(8,128)S(1)} %collective-permute-done.6.yo, f32[4,176,256]{2,1,0:T(8,128)S(1)} %slope_middle.1.slope, f32[2,176,256]{2,1,0:T(8,128)S(1)} %slope_sides.1.outer, ...), custom_call_target="tpu_custom_call" | custom-call | flops 2000000000 | bytes 4194304 | tf_op jit(solution)/shard_map/gradient_sides/pallas_call | solution.py:585
Async XLA Ops:
  6.1 8.5 %collective-permute-start.1 = (f32[888,128]{1,0:T(8,128)S(1)}, f32[888,128]{1,0:T(8,128)S(1)}, u32[]{:S(2)}, u32[]{:S(2)}) collective-permute-start(f32[888,128]{1,0:T(8,128)S(1)} %get-tuple-element.20), channel_id=1, source_target_pairs={{0,1},{1,0},{2,3},{3,2},{4,5},{5,4},{6,7},{7,6},{8,9},{9,8},{10,11... | collective-permute-start | bytes 1363976 | tf_op jit(solution)/shard_map/ppermute | solution.py:463
  11.4 7.5 %collective-permute-start = (f32[600,128]{1,0:T(8,128)S(1)}, f32[600,128]{1,0:T(8,128)S(1)}, u32[]{:S(2)}, u32[]{:S(2)}) collective-permute-start(f32[600,128]{1,0:T(8,128)S(1)} %get-tuple-element.19), channel_id=1, source_target_pairs={{0,16},{1,17},{2,18},{3,19},{4,20},{5,21},{6,22},{7,23},{8,24},{9,... | collective-permute-start | bytes 921608 | tf_op jit(solution)/shard_map/ppermute | solution.py:463
  11.8 1.5 %collective-permute-start.2 = (f32[2,144,128]{2,1,0:T(8,128)S(1)}, f32[2,144,128]{2,1,0:T(8,128)S(1)}, u32[]{:S(2)}, u32[]{:S(2)}) collective-permute-start(f32[2,144,128]{2,1,0:T(8,128)S(1)} %get-tuple-element.22), channel_id=1, source_target_pairs={{0,16},{1,17},{2,18},{3,19},{4,20},{5,21},{6,22},{7,23},{8,24},{9,... | collective-permute-start | bytes 442376 | tf_op jit(solution)/shard_map/ppermute | solution.py:463
  15.2 6.4 %copy-start = (bf16[1536,256]{1,0:T(8,128)(2,1)S(1)}, bf16[1536,256]{1,0:T(8,128)(2,1)}, u32[]{:S(2)}) copy-start(bf16[1536,256]{1,0:T(8,128)(2,1)} %constant.4.clone.high_ref) | copy-start | bytes 2359300
  15.2 6.4 %copy-start.1 = (bf16[1536,256]{1,0:T(8,128)(2,1)S(1)}, bf16[1536,256]{1,0:T(8,128)(2,1)}, u32[]{:S(2)}) copy-start(bf16[1536,256]{1,0:T(8,128)(2,1)} %constant.5.clone.low_ref) | copy-start | bytes 2359300
  15.2 8.7 %collective-permute-start.3 = (f32[272,128]{1,0:T(8,128)S(1)}, f32[272,128]{1,0:T(8,128)S(1)}, u32[]{:S(2)}, u32[]{:S(2)}) collective-permute-start(f32[272,128]{1,0:T(8,128)S(1)} %get-tuple-element.23), channel_id=1, source_target_pairs={{0,1},{1,0},{2,3},{3,2},{4,5},{5,4},{6,7},{7,6},{8,9},{9,8},{10,11... | collective-permute-start | bytes 417800 | tf_op jit(solution)/shard_map/ppermute | solution.py:463
  16.8 7.6 %collective-permute-start.4 = (f32[272,128]{1,0:T(8,128)S(1)}, f32[272,128]{1,0:T(8,128)S(1)}, u32[]{:S(2)}, u32[]{:S(2)}) collective-permute-start(f32[272,128]{1,0:T(8,128)S(1)} %get-tuple-element.24), channel_id=1, source_target_pairs={{0,16},{1,2},{2,1},{3,4},{4,3},{5,6},{6,5},{7,8},{8,7},{9,10},{10,... | collective-permute-start | bytes 417800 | tf_op jit(solution)/shard_map/ppermute | solution.py:463
  19.4 7.7 %collective-permute-start.5 = (f32[232,128]{1,0:T(8,128)S(1)}, f32[232,128]{1,0:T(8,128)S(1)}, u32[]{:S(2)}, u32[]{:S(2)}) collective-permute-start(f32[232,128]{1,0:T(8,128)S(1)} %get-tuple-element.26), channel_id=1, source_target_pairs={{0,1},{1,0},{2,3},{3,2},{4,5},{5,4},{6,7},{7,6},{8,9},{9,8},{10,11... | collective-permute-start | bytes 356360 | tf_op jit(solution)/shard_map/ppermute | solution.py:463
  20.1 6.9 %collective-permute-start.6 = (f32[232,128]{1,0:T(8,128)S(1)}, f32[232,128]{1,0:T(8,128)S(1)}, u32[]{:S(2)}, u32[]{:S(2)}) collective-permute-start(f32[232,128]{1,0:T(8,128)S(1)} %get-tuple-element.27), channel_id=1, source_target_pairs={{0,16},{1,2},{2,1},{3,4},{4,3},{5,6},{6,5},{7,8},{8,7},{9,10},{10,... | collective-permute-start | bytes 356360 | tf_op jit(solution)/shard_map/ppermute | solution.py:463
